TPU v7x, 32 devices: a whole 2x2x4 slice. The times are simulated.
32 devices in a mesh: coarse: 2 (over x), fine: 4 (over y, core), swath: 4 (over z).
Axes of the slice: x: 2, y: 2, z: 4, core: 2. Of those that a mesh axis runs over, the one named last changes fastest.
Arguments:
- echoes: int32 [32, 64, 2, 2048], P(('coarse', 'fine'), None, None, 'swath'), may hold values from -127 to 127
- exponents: int32 [32, 64, 64], P(('coarse', 'fine'), None, 'swath'), may hold values from 0 to 3
- replica: bfloat16 [2, 129], replicated, may hold values from -0.375 to 0.375
- interp0: bfloat16 [2, 32, 64, 64], P(None, ('coarse', 'fine')), may hold values from -0.5 to 0.5
- upsample1: bfloat16 [2, 32, 64, 512], P(None, ('coarse', 'fine')), may hold values from -0.1875 to 0.1875
- phase1: bfloat16 [512, 32, 2048], P(None, ('coarse', 'fine'), 'swath'), may hold values from -3.140625 to 3.140625
- upsample2: bfloat16 [4, 2, 512, 2048], P('coarse', None, 'fine'), may hold values from -0.09375 to 0.09375
- phase2: bfloat16 [2048, 4, 2048], P(None, 'coarse', 'swath'), may hold values from -3.140625 to 3.140625
Outputs:
- image: float32 [2048, 2, 2048], P(('coarse', 'fine'), None, 'swath')
All inputs are finite; a program needn't handle non-finite values.
Results may differ from a plain program's by a relative error of at most 0.005.
Values may be sent and summed in bfloat16 or wider, within the bound.
A program may use at most 128 MiB of HBM per device.

v0:
```python
import jax
import jax.numpy as jnp
from jax import lax
from jax.sharding import PartitionSpec as P


def with_halo(shard, sides, width):
    for axis, dim in sides:
        size, length = (lax.axis_size(axis), shard.shape[dim])
        up = [(i, (i + 1) % size) for i in range(size - 1)]
        down = [(j, i) for i, j in up]
        last = lax.slice_in_dim(shard, length - width, length, axis=dim)
        first = lax.slice_in_dim(shard, 0, width, axis=dim)
        before = lax.ppermute(last, axis, up)
        after = lax.ppermute(first, axis, down)
        shard = jnp.concatenate([before, shard, after], axis=dim)
    return shard


def band_matrix(taps, window, out_bins):
    line = jnp.concatenate([taps, jnp.zeros((window + 1 - taps.shape[0],), taps.dtype)])
    flat = jnp.tile(line, out_bins)[: out_bins * window]
    return flat.reshape(out_bins, window).T


def complex_mixer(real_part, imag_part):
    first = jnp.stack([real_part, imag_part], axis=-2)
    second = jnp.stack([-imag_part, real_part], axis=-2)
    return jnp.stack([first, second], axis=1)


def rotate(values, angles):
    radians = angles.astype(jnp.float32)
    cosine = jnp.cos(radians)
    sine = jnp.sin(radians)
    real_out = cosine * values[:, 0] - sine * values[:, 1]
    imag_out = sine * values[:, 0] + cosine * values[:, 1]
    return jnp.stack([real_out, imag_out], axis=1)


def second_term(weight_table, children, angle_rows):
    real_part = weight_table[:, 0]
    imag_part = weight_table[:, 1]
    mixer = complex_mixer(real_part, imag_part)
    turned = jnp.einsum("gibon,bigr->nogr", mixer, children, preferred_element_type=jnp.float32)
    rotated = rotate(turned, angle_rows)
    return jnp.sum(rotated, axis=2)


def shards(echoes, exponents, replica, interp0, upsample1, phase1, upsample2, phase2):
    sub_count = echoes.shape[0]
    ping_count = echoes.shape[1]
    range_bins = echoes.shape[3]
    group_count = upsample2.shape[0]
    kid_count = sub_count // group_count
    half_taps = (replica.shape[1] - 1) // 2
    quant_block = range_bins // exponents.shape[2]
    factors = jnp.repeat(jnp.exp2(exponents.astype(jnp.float32) - 8.0), quant_block, axis=2)
    samples = (echoes.astype(jnp.float32) * factors[:, :, None, :]).astype(jnp.bfloat16)
    padded = with_halo(samples, (("swath", 3),), half_taps)
    tile_bins = 128
    tile_count = range_bins // tile_bins
    window = tile_bins + 2 * half_taps
    real_band = band_matrix(replica[0], window, tile_bins)
    imag_band = band_matrix(replica[1], window, tile_bins)
    kernel = jnp.concatenate(
        [
            jnp.concatenate([real_band, -imag_band], axis=1),
            jnp.concatenate([imag_band, real_band], axis=1),
        ],
        axis=0,
    )
    pieces = []
    for tile in range(tile_count):
        segment = padded[:, :, :, tile * tile_bins : tile * tile_bins + window]
        product = jnp.dot(
            segment.reshape(sub_count * ping_count, 2 * window),
            kernel,
            preferred_element_type=jnp.float32,
        )
        pieces.append(product.astype(jnp.bfloat16).reshape(sub_count, ping_count, 2, tile_bins))
    compressed = jnp.concatenate(pieces, axis=3)
    mixer_zero = complex_mixer(interp0[0], interp0[1])
    beams = jnp.einsum(
        "silob,slir->sobr", mixer_zero, compressed, preferred_element_type=jnp.float32
    ).astype(jnp.bfloat16)
    local_rows = upsample1.shape[3] // lax.axis_size("fine")
    real_part = upsample1[0]
    imag_part = upsample1[1]
    mixer = complex_mixer(real_part, imag_part)
    turned = jnp.einsum("sibon,sibr->nosr", mixer, beams, preferred_element_type=jnp.float32)
    rotated = rotate(turned, phase1)
    level_one = lax.psum_scatter(
        jnp.sum(
            rotated.reshape(
                lax.axis_size("fine") * local_rows, 2, group_count, kid_count, range_bins
            ),
            axis=3,
        ),
        "fine",
        scatter_dimension=0,
        tiled=True,
    ).astype(jnp.bfloat16)
    fine_count = lax.axis_size("fine")
    coarse_count = lax.axis_size("coarse")
    wedge = upsample2.shape[3] // (coarse_count * fine_count)
    children = lax.all_gather(level_one, "fine", axis=0, tiled=True)
    shaped = upsample2.reshape(group_count, 2, upsample2.shape[2], coarse_count, fine_count, wedge)
    columns = lax.all_to_all(shaped, "fine", split_axis=4, concat_axis=2, tiled=True)
    columns = columns.reshape(group_count, 2, children.shape[0], coarse_count * wedge)
    phase_split = phase2.reshape(coarse_count, fine_count, wedge, group_count, range_bins)
    angle_rows = lax.dynamic_index_in_dim(phase_split, lax.axis_index("fine"), 1, keepdims=False)
    angle_rows = angle_rows.reshape(coarse_count * wedge, group_count, range_bins)
    return lax.psum_scatter(
        second_term(columns, children, angle_rows), "coarse", scatter_dimension=0, tiled=True
    )


def solution(mesh):
    in_specs = (
        P(("coarse", "fine"), None, None, "swath"),
        P(("coarse", "fine"), None, "swath"),
        P(),
        P(None, ("coarse", "fine"), None, None),
        P(None, ("coarse", "fine"), None, None),
        P(None, ("coarse", "fine"), "swath"),
        P("coarse", None, "fine", None),
        P(None, "coarse", "swath"),
    )
    out_specs = P(("coarse", "fine"), None, "swath")
    return jax.shard_map(shards, mesh=mesh, in_specs=in_specs, out_specs=out_specs, check_vma=False)
```

profile of v0, /device:TPU:0, one launch (start us, length us, event | category | flops | bytes accessed | tf_op | source)
XLA Modules:
  0.0 242.9 jit_solution(16916185704481502255)
XLA Ops:
  6.5 0.8 multiply_exponential_fusion
  7.7 1.8 multiply_convert_fusion
  9.5 0.9 fusion.32
  10.4 5.6 %collective-permute-start = (bf16[4,64,2,64]{3,2,1,0:T(2,128)(2,1)}, bf16[4,64,2,64]{3,2,1,0:T(2,128)(2,1)}, u32[]{:S(2)}, u32[]{:S(2)}) collective-permute-start(bf16[4,64,2,64]{3,2,1,0:T(2,128)(2,1)} %get-tuple-element.21), channel_id=1, source_target_pairs={{0,1},{1,2},{2,3},{4,5},{5,6},{6,7},{8,9},{9,10},{10,11},{12,13},{... | collective-permute-start | bytes 196616 | tf_op jit(solution)/shard_map/ppermute | solution.py:14
  16.0 1.3 collective-permute-start.1
  17.3 0.9 slice_bitcast_fusion.4
  18.7 0.6 bitcast_negate_fusion
  19.7 0.6 reshape.105
  20.5 0.7 copy.64
  21.2 3.0 %copy.40 = bf16[512,4,512]{0,2,1:T(8,128)(2,1)S(1)} copy(bf16[512,4,512]{2,1,0:T(4,128)(2,1)} %param.13) | data formatting | bytes 4194304 | tf_op args[5]
  24.2 2.0 maximum_bitcast_fusion.4
  26.2 1.7 maximum_bitcast_fusion.6
  27.9 3.4 %pad_maximum_fusion.1 = (bf16[4,64,2,256]{3,2,1,0:T(2,128)(2,1)S(1)}, bf16[4,64,2,256]{3,2,1,0:T(2,128)(2,1)}, bf16[4,64,2,256]{3,2,1,0:T(2,128)(2,1)}, bf16[4,64,2,256]{3,2,1,0:T(2,128)(2,1)S(1)}) fusion(bf16[4,64,2,512]{3,2,1,0:T(2,128)(2,1)S(1)} %multiply_convert_fusion, bf16[4,64,2,64]{3,2,1,0:T(2,128)(2,1)} %collective-permute-done, ...), kind=kLoop, calls=%fused_computation.48 | loop fusion | flops 1048576 | bytes 2228224 | tf_op jit(solution)/shard_map/concatenate | solution.py:16
  31.3 0.9 convolution_convert_fusion.3
  32.3 0.9 reshape.107
  33.2 0.7 copy.44
  33.9 1.2 convolution_convert_fusion.2
  35.2 0.7 copy.45
  35.9 1.2 convolution_convert_fusion.1
  37.1 0.7 copy.46
  37.8 1.2 convolution_convert_fusion
  39.1 1.5 fusion.19
  40.6 1.3 convolution_bitcast_fusion
  41.9 15.5 %fusion.4 = (f32[512,4,512]{0,2,1:T(8,128)S(1)}, f32[512,4,512]{0,2,1:T(8,128)S(1)}) fusion(bf16[512,4,512]{0,2,1:T(8,128)(2,1)S(1)} %copy.40, f32[512,2,4,512]{0,3,1,2:T(8,128)S(1)} %convolution_bitcast_fusion), kind=kLoop, calls=%fused_computation.7 | loop fusion | flops 7340032 | bytes 18874368 | tf_op jit(solution)/shard_map/sub | solution.py:36
  57.4 1.2 maximum_reduce_fusion
  58.7 2.4 copy.50
  61.1 46.9 %reduce-scatter.2.cloned.1.call-done = f32[128,2,2,512]{0,3,1,2:T(8,128)} async-done(((f32[512,2,2,512]{0,3,1,2:T(8,128)}), f32[128,2,2,512]{0,3,1,2:T(8,128)}) %reduce-scatter.2.cloned.1.call-update) | async-done | bytes 1048592 | tf_op jit(solution)/shard_map/reduce_scatter | solution.py:93
  108.0 2.1 convert_element_type.55
  110.2 3.0 %copy.51 = bf16[2,2,128,2048]{2,3,1,0:T(8,128)(2,1)S(1)} copy(bf16[2,2,128,2048]{3,2,1,0:T(8,128)(2,1)} %param.14) | data formatting | bytes 4194304 | tf_op args[6]
  113.2 3.8 %copy.52 = bf16[2,2,128,2,4,256]{5,3,2,0,1,4:T(2,128)(2,1)} copy(bf16[2,2,128,2,4,256]{2,5,4,3,1,0:T(8,128)(2,1)S(1)} %bitcast.117) | data formatting | bytes 4194304 | tf_op jit(solution)/shard_map/reshape | solution.py:108
  117.1 3.6 %all-to-all-start = ((bf16[2,2,128,2,4,256]{5,3,2,0,1,4:T(2,128)(2,1)}), bf16[2,2,128,2,4,256]{5,3,2,0,1,4:T(2,128)(2,1)S(1)}, u32[]{:S(2)}, u32[]{:S(2)}) async-start(bf16[2,2,128,2,4,256]{5,3,2,0,1,4:T(2,128)(2,1)} %copy.52), calls=%async_computation.1 | async-start | bytes 4194304 | tf_op jit(solution)/shard_map/all_to_all | solution.py:109
  120.9 2.9 %constant_dynamic-slice_fusion.1 = bf16[2,1,256,2,512]{4,3,2,1,0:T(2,128)(2,1)} fusion(bf16[2,4,256,2,512]{4,3,2,1,0:T(2,128)(2,1)} %bitcast.125, s32[]{:T(128)S(6)} %select_n.4), kind=kLoop, calls=%fused_computation.60 | loop fusion | bytes 2097156 | tf_op jit(solution)/shard_map/jit(dynamic_index_in_dim)/dynamic_slice | solution.py:112
  123.8 4.8 %copy.63 = bf16[2,1,256,2,512]{2,0,4,3,1:T(2,128)(2,1)S(1)} copy(bf16[2,1,256,2,512]{4,3,2,1,0:T(2,128)(2,1)} %constant_dynamic-slice_fusion.1) | data formatting | bytes 2097152
  128.7 8.3 %convert_sine_fusion.1 = (f32[8,1,256,2,128]{2,0,4,3,1:T(8,128)}, f32[8,1,256,2,128]{2,0,4,3,1:T(8,128)}) fusion(bf16[8,1,256,2,128]{2,0,4,3,1:T(8,128)(2,1)S(1)} %bitcast.118), kind=kLoop, calls=%fused_computation.17 | loop fusion | flops 524288 | bytes 5242880 | tf_op jit(solution)/shard_map/sin | solution.py:35
  137.0 3.9 %cos.18 = f32[512,1,2,512]{0,3,1,2:T(8,128)} reshape(f32[2,1,256,2,512]{2,0,4,3,1:T(2,128)} %bitcast.116) | data formatting | bytes 4194304 | tf_op jit(solution)/shard_map/cos | solution.py:34
  140.8 3.9 %sin.19 = f32[512,1,2,512]{0,3,1,2:T(8,128)} reshape(f32[2,1,256,2,512]{2,0,4,3,1:T(2,128)} %bitcast.115) | data formatting | bytes 4194304 | tf_op jit(solution)/shard_map/sin | solution.py:35
  144.8 9.1 %all-to-all-done = bf16[2,2,128,2,4,256]{5,3,2,0,1,4:T(2,128)(2,1)S(1)} async-done(((bf16[2,2,128,2,4,256]{5,3,2,0,1,4:T(2,128)(2,1)}), bf16[2,2,128,2,4,256]{5,3,2,0,1,4:T(2,128)(2,1)S(1)}, u32[]{:S(2)}, u32[]{:S(2)}) %all-to-all-start) | async-done | bytes 2097184 | tf_op jit(solution)/shard_map/all_to_all | solution.py:109
  153.8 2.9 %copy.53 = bf16[2,2,4,128,2,1,256]{6,4,3,2,0,1,5:T(2,128)(2,1)} copy(bf16[2,2,4,128,2,1,256]{6,4,3,0,1,2,5:T(2,128)(2,1)S(1)} %bitcast.114) | data formatting | bytes 4194304 | tf_op jit(solution)/shard_map/all_to_all | solution.py:109
  156.8 3.2 %reshape.115 = bf16[2,2,512,512]{3,2,0,1:T(8,128)(2,1)S(1)} reshape(bf16[2,2,4,128,2,1,256]{6,4,3,2,0,1,5:T(2,128)(2,1)} %copy.53) | data formatting | bytes 4194304 | tf_op jit(solution)/shard_map/reshape | solution.py:110
  160.2 1.7 maximum_bitcast_fusion
  161.9 4.7 %fusion.10 = f32[512,2,2,512]{0,3,1,2:T(8,128)S(1)} fusion(bf16[2,1,512,2,512]{4,2,1,3,0:T(8,128)(2,1)} %get-tuple-element.14, bf16[2,1,512,2,512]{4,2,1,3,0:T(8,128)(2,1)S(1)} %get-tuple-element.13, bf16[512,2,2,512]{0,3,1,2:T(8,128)(2,1)} %all-gather.2.cloned.1.call-done), kind=kOutput, calls=%fused_computation.19 | convolution fusion | flops 2155872256 | bytes 10485760 | tf_op jit(solution)/shard_map/gibon,bigr->nogr/dot_general | solution.py:45
  166.6 1.0 multiply_subtract_fusion
  167.7 0.6 maximum_reduce_fusion.1
  168.2 2.4 %copy.55 = f32[512,2,512]{2,1,0:T(2,128)} copy(f32[512,2,512]{0,2,1:T(8,128)S(1)} %maximum_reduce_fusion.1) | data formatting | bytes 4194304 | tf_op jit(solution)/shard_map/reduce_sum | solution.py:47
  170.7 0.6 copy-done.14
  171.3 0.6 dynamic-slice
  172.6 61.2 %all-reduce.5.cloned.1.call-done = f32[512,2,512]{2,1,0:T(2,128)} async-done(((f32[512,2,512]{2,1,0:T(2,128)}), f32[512,2,512]{2,1,0:T(2,128)}) %all-reduce.5.cloned.1.call-update) | async-done | bytes 2097168
  233.8 2.6 %constant_dynamic-slice_fusion = f32[256,2,512]{2,1,0:T(2,128)} fusion(f32[512,2,512]{2,1,0:T(2,128)} %all-reduce.5.cloned.1.call-done, u32[]{:T(128)S(6)} %multiply.1), kind=kLoop, calls=%fused_computation.59 | loop fusion | bytes 2097156
  (64 shorter events, 2.2 us)
Async XLA Ops:
  6.5 101.5 %reduce-scatter.2.cloned.1.call-start = ((), (), s32[]{:S(2)}) async-start(), calls=%async_computation.2 | async-start | bytes 5242880 | tf_op jit(solution)/shard_map/reduce_scatter | solution.py:93
  7.4 9.9 %copy-start.3 = (bf16[2,4,64,512]{3,2,1,0:T(8,128)(2,1)S(1)}, bf16[2,4,64,512]{3,2,1,0:T(8,128)(2,1)}, u32[]{:S(2)}) copy-start(bf16[2,4,64,512]{3,2,1,0:T(8,128)(2,1)} %param.12) | copy-start | bytes 1572868
  7.7 10.5 %copy-start.13 = (bf16[2,129]{1,0:T(2,128)(2,1)S(1)}, bf16[2,129]{1,0:T(2,128)(2,1)}, u32[]{:S(2)}) copy-start(bf16[2,129]{1,0:T(2,128)(2,1)} %param.10) | copy-start | bytes 1552
  9.5 10.8 %copy-start.9 = (bf16[2,4,64,64]{3,2,1,0:T(8,128)(2,1)S(1)}, bf16[2,4,64,64]{3,2,1,0:T(8,128)(2,1)}, u32[]{:S(2)}) copy-start(bf16[2,4,64,64]{3,2,1,0:T(8,128)(2,1)} %param.11) | copy-start | bytes 196612
  10.4 17.4 %collective-permute-start = (bf16[4,64,2,64]{3,2,1,0:T(2,128)(2,1)}, bf16[4,64,2,64]{3,2,1,0:T(2,128)(2,1)}, u32[]{:S(2)}, u32[]{:S(2)}) collective-permute-start(bf16[4,64,2,64]{3,2,1,0:T(2,128)(2,1)} %get-tuple-element.21), channel_id=1, source_target_pairs={{0,1},{1,2},{2,3},{4,5},{5,6},{6,7},{8,9},{9,10},{10,11},{12,13},{... | collective-permute-start | bytes 196616 | tf_op jit(solution)/shard_map/ppermute | solution.py:14
  16.0 11.8 %collective-permute-start.1 = (bf16[4,64,2,64]{3,2,1,0:T(2,128)(2,1)}, bf16[4,64,2,64]{3,2,1,0:T(2,128)(2,1)}, u32[]{:S(2)}, u32[]{:S(2)}) collective-permute-start(bf16[4,64,2,64]{3,2,1,0:T(2,128)(2,1)} %get-tuple-element.22), channel_id=1, source_target_pairs={{1,0},{2,1},{3,2},{5,4},{6,5},{7,6},{9,8},{10,9},{11,10},{13,12},{... | collective-permute-start | bytes 196616 | tf_op jit(solution)/shard_map/ppermute | solution.py:15
  18.6 0.7 copy-start.6
  26.2 5.1 %copy-start.7 = (bf16[128,256]{1,0:T(8,128)(2,1)S(1)}, bf16[128,256]{1,0:T(8,128)(2,1)}, u32[]{:S(2)}) copy-start(bf16[128,256]{1,0:T(8,128)(2,1)} %copy-done.6) | copy-start | bytes 196612
  26.2 5.1 %copy-start.10 = (bf16[256,128]{0,1:T(8,128)(2,1)S(1)}, bf16[256,128]{0,1:T(8,128)(2,1)}, u32[]{:S(2)}) copy-start(bf16[256,128]{0,1:T(8,128)(2,1)} %bitcast_negate_fusion) | copy-start | bytes 196612
  26.2 5.1 %copy-start.12 = (bf16[128,256]{1,0:T(8,128)(2,1)S(1)}, bf16[128,256]{1,0:T(8,128)(2,1)}, u32[]{:S(2)}) copy-start(bf16[128,256]{1,0:T(8,128)(2,1)} %reshape.105) | copy-start | bytes 196612
  31.3 2.6 %copy-start.5 = (bf16[4,64,2,256]{3,2,1,0:T(2,128)(2,1)S(1)}, bf16[4,64,2,256]{3,2,1,0:T(2,128)(2,1)}, u32[]{:S(2)}) copy-start(bf16[4,64,2,256]{3,2,1,0:T(2,128)(2,1)} %get-tuple-element.19) | copy-start | bytes 786436
  31.3 4.6 %copy-start.4 = (bf16[4,64,2,256]{3,2,1,0:T(2,128)(2,1)S(1)}, bf16[4,64,2,256]{3,2,1,0:T(2,128)(2,1)}, u32[]{:S(2)}) copy-start(bf16[4,64,2,256]{3,2,1,0:T(2,128)(2,1)} %get-tuple-element.18) | copy-start | bytes 786436
  33.9 2.0 copy-start.8
  33.9 2.0 copy-start.11
  37.8 2.8 %copy-start.2 = (bf16[4,1,64,2,512]{4,2,1,3,0:T(8,128)(2,1)S(1)}, bf16[4,1,64,2,512]{4,2,1,3,0:T(8,128)(2,1)}, u32[]{:S(2)}) copy-start(bf16[4,1,64,2,512]{4,2,1,3,0:T(8,128)(2,1)} %get-tuple-element.26) | copy-start | bytes 1572868
  61.1 100.8 %all-gather.2.cloned.1.call-start = ((), (), s32[]{:S(2)}) async-start(), calls=%async_computation.3 | async-start | bytes 2621440 | tf_op jit(solution)/shard_map/all_gather | solution.py:107
  117.1 36.8 %all-to-all-start = ((bf16[2,2,128,2,4,256]{5,3,2,0,1,4:T(2,128)(2,1)}), bf16[2,2,128,2,4,256]{5,3,2,0,1,4:T(2,128)(2,1)S(1)}, u32[]{:S(2)}, u32[]{:S(2)}) async-start(bf16[2,2,128,2,4,256]{5,3,2,0,1,4:T(2,128)(2,1)} %copy.52), calls=%async_computation.1 | async-start | bytes 4194304 | tf_op jit(solution)/shard_map/all_to_all | solution.py:109
  120.7 113.1 %all-reduce.5.cloned.1.call-start = ((), (), s32[]{:S(2)}) async-start(), calls=%async_computation.4 | async-start | bytes 4194304
  161.9 4.7 %copy-start = (f32[512,1,2,512]{0,3,1,2:T(8,128)S(1)}, f32[512,1,2,512]{0,3,1,2:T(8,128)}, u32[]{:S(2)}) copy-start(f32[512,1,2,512]{0,3,1,2:T(8,128)} %cos.18) | copy-start | bytes 6291460
  161.9 4.7 %copy-start.1 = (f32[512,1,2,512]{0,3,1,2:T(8,128)S(1)}, f32[512,1,2,512]{0,3,1,2:T(8,128)}, u32[]{:S(2)}) copy-start(f32[512,1,2,512]{0,3,1,2:T(8,128)} %sin.19) | copy-start | bytes 6291460
  170.7 0.7 copy-start.14
Sparse Core Ops, SparseCore 0:
  61.2 46.8 reduce-scatter.1
  110.3 30.3 all-gather.1
  170.8 62.9 all-reduce.4
where the time goes:
time: 244 us; the launch traced here: 243 us
  waiting for transfers between devices  117 us (48%)
  local copies, waits for them, and re-layouts  47.8 us (20%)
  other arithmetic  40.8 us (17%)
  between operations  14.2 us (6%)
  matrix products  12 us (5%)
  starting transfers between devices  10.7 us (4%)
    unnamed x4, waiting for transfers between devices  61.3 us
    reduce_scatter x1, waiting for transfers between devices, shards(): lax.psum_scatter(jnp.sum(rotated.reshape(lax.axis_size('fine') * local_ro...  46.9 us
    sub x2, other arithmetic, rotate(): real_out = cosine * values[:, 0] - sine * values[:, 1]  16.5 us
    unnamed x41, local copies, waits for them, and re-layouts  15.6 us
    all_to_all x1, waiting for transfers between devices, shards(): lax.all_to_all(shaped, 'fine', split_axis=4, concat_axis=2, tiled=True)  9.09 us
    sin x1, other arithmetic, rotate(): sine = jnp.sin(radians)  8.3 us
    ppermute x1, starting transfers between devices, with_halo(): before = lax.ppermute(last, axis, up)  5.58 us
    another operation x3, other arithmetic, complex_mixer(): return jnp.stack([first, second], axis=1)  5.41 us
  transfers between devices with their start and end apart: 6, of which 3 were waited for; matrix products, arithmetic and copies ran while one was open for 20% of the time, Pallas kernels for 0%

commit v1 on v0

v1 whole, which is shorter than its diff:
```python
import functools

import jax
import jax.numpy as jnp
from jax import lax
from jax.experimental import pallas as pl
from jax.experimental.pallas import tpu as pltpu
from jax.sharding import PartitionSpec as P

MESH = pl.DeviceIdType.MESH
CHUNK = 128

SIN = (0.7071067690849304, -0.029462767764925957, 0.0003682722744997591, -2.1886112335778307e-06, 7.1958234926228215e-09)
COS = (1.4142135381698608, -0.17677636444568634, 0.0036825749557465315, -3.061256938963197e-05, 1.2790442838195304e-07)


def horner(coefs, u):
    total = coefs[-1] * u + coefs[-2]
    for coef in coefs[-3::-1]:
        total = total * u + coef
    return total


def cos_sin(angles):
    x = angles.astype(jnp.float32)
    u = x * x
    s = x * horner(SIN, u)
    c = horner(COS, u)
    return 1.0 - s * s, s * c


def mixed(values):
    re = values[:, :CHUNK]
    im = values[:, CHUNK:]
    return jnp.concatenate([values, jnp.concatenate([-im, re], axis=1)], axis=0)


def turned(values, angles):
    cosine, sine = cos_sin(angles)
    re = values[:, :CHUNK]
    im = values[:, CHUNK:]
    return cosine * re - sine * im, sine * re + cosine * im


def dot(a, b):
    return jnp.dot(a, b, preferred_element_type=jnp.float32)


def kernel(
    dims, samples, taps, w0, w1, ph1, u2, ph2, out,
    xs, halo_l, halo_r, band, rhs1, rhs2, u2m, pown, pms, pmr, ys, yr, lown, lmr, xsnd, xrcv, iown, y2s, y2r,
    u2_sem, halo_sem, core_sem, y_sem, l_sem, x_sem, y2_sem,
):
    C, Y, Z, G, K, S, L, B0, nb, wedge, NB, half = dims
    W = CHUNK
    R = NB * W
    c = lax.axis_index("coarse")
    f = lax.axis_index("fine")
    z = lax.axis_index("swath")
    y = f // 2
    k = f % 2
    mate = {"fine": y * 2 + 1 - k}

    def y_peer(d):
        return {"fine": ((y + d) % Y) * 2 + k}

    def x_peer(e):
        return {"coarse": (c + e) % C}

    barrier = pltpu.get_barrier_semaphore()
    partners = [mate] + [y_peer(d) for d in range(1, Y)] + [x_peer(e) for e in range(1, C)]
    for who in partners:
        pl.semaphore_signal(barrier, inc=1, device_id=who, device_id_type=MESH)

    @pl.when(z < Z - 1)
    def _():
        pl.semaphore_signal(barrier, inc=1, device_id={"swath": z + 1}, device_id_type=MESH)

    @pl.when(z > 0)
    def _():
        pl.semaphore_signal(barrier, inc=1, device_id={"swath": z - 1}, device_id_type=MESH)

    ends = jnp.where(z > 0, 1, 0) + jnp.where(z < Z - 1, 1, 0)
    pl.semaphore_wait(barrier, len(partners) + ends)

    def remote(src, dst, sems, who):
        return pltpu.make_async_remote_copy(
            src_ref=src, dst_ref=dst, send_sem=sems.at[0], recv_sem=sems.at[1], device_id=who, device_id_type=MESH
        )

    right = remote(samples.at[:, :, R - W : R], halo_l, halo_sem.at[0], {"swath": jnp.minimum(z + 1, Z - 1)})
    left = remote(samples.at[:, :, 0:W], halo_r, halo_sem.at[1], {"swath": jnp.maximum(z - 1, 0)})

    @pl.when(z < Z - 1)
    def _():
        right.start()

    @pl.when(z > 0)
    def _():
        left.start()

    u2_copy = remote(u2.at[1 - k], u2m, u2_sem, mate)
    u2_copy.start()
    sent = [u2_copy]

    reach = 3 * W
    width = taps.shape[1]
    toeplitz = []
    for part in range(2):
        row = jnp.broadcast_to(taps[part : part + 1, :], (reach, width))
        rolled = pltpu.roll(row, (half - W) % width, 1, stride=1, stride_axis=0)
        toeplitz.append(rolled[:, :W].astype(jnp.bfloat16))
    band[0, :, :W] = toeplitz[0]
    band[0, :, W:] = -toeplitz[1]
    band[1, :, :W] = toeplitz[1]
    band[1, :, W:] = toeplitz[0]
    xs[:, :, W : W + R] = samples[...]

    def fill_halo():
        @pl.when(z > 0)
        def _():
            right.wait_recv()
            xs[:, :, 0:W] = halo_l[...]

        @pl.when(z == 0)
        def _():
            xs[:, :, 0:W] = jnp.zeros((2, S * L, W), jnp.bfloat16)

        @pl.when(z < Z - 1)
        def _():
            left.wait_recv()
            xs[:, :, W + R : R + 2 * W] = halo_r[...]

        @pl.when(z == Z - 1)
        def _():
            xs[:, :, W + R : R + 2 * W] = jnp.zeros((2, S * L, W), jnp.bfloat16)

    core_copy, y_copy, l_copy, x_copy, y2_copy = {}, {}, {}, {}, {}
    sb1 = min(nb, 64)
    sb2 = min(wedge, 64)

    def level_one(j, nth):
        lanes = pl.ds(j * W, W)
        window = pl.ds(j * W, reach)
        comp = (dot(xs[0, :, window], band[0]) + dot(xs[1, :, window], band[1])).astype(jnp.bfloat16)
        for s in range(S):
            beams = dot(w0[s], mixed(comp[s * L : (s + 1) * L])).astype(jnp.bfloat16)
            rhs1[s] = mixed(beams)
        subs = nb // sb1

        def block(core, t):
            d = t // (G * subs)
            g = (t // subs) % G
            start = (t % subs) * sb1
            rows = pl.ds(pl.multiple_of((((y + d) % Y) * 2 + core) * nb + start, sb1), sb1)
            re = im = 0.0
            for kid in range(K):
                s = g * K + kid
                r, i = turned(dot(w1[s, rows, :], rhs1[s]), ph1[s, rows, lanes])
                re = re + r
                im = im + i
            return d, g, pl.ds(pl.multiple_of(start, sb1), sb1), re, im

        @pl.loop(0, Y * G * subs)
        def _(t):
            d, g, rows, re, im = block(1 - k, t)
            pms[nth, d, g, rows, :W] = re.astype(jnp.bfloat16)
            pms[nth, d, g, rows, W:] = im.astype(jnp.bfloat16)

        copy = remote(pms.at[nth], pmr.at[nth], core_sem.at[nth], mate)
        copy.start()
        core_copy[nth] = copy

        @pl.loop(0, Y * G * subs)
        def _(t):
            d, g, rows, re, im = block(k, t)
            pown[nth, d, g, rows, :W] = re
            pown[nth, d, g, rows, W:] = im

    def sum_cores(nth):
        core_copy[nth].wait_recv()
        for d in range(1, Y):
            for g in range(G):
                ys[nth, d - 1, g] = (pown[nth, d, g] + pmr[nth, d, g].astype(jnp.float32)).astype(jnp.bfloat16)
            copy = remote(ys.at[nth, d - 1], yr.at[nth, d - 1], y_sem.at[nth, d - 1], y_peer(d))
            copy.start()
            y_copy[nth, d] = copy

    def sum_y(nth):
        for d in range(1, Y):
            y_copy[nth, d].wait_recv()
        for g in range(G):
            total = pown[nth, 0, g] + pmr[nth, 0, g].astype(jnp.float32)
            for d in range(1, Y):
                total = total + yr[nth, d - 1, g].astype(jnp.float32)
            lown[nth, g] = total.astype(jnp.bfloat16)
        copy = remote(lown.at[nth], lmr.at[nth], l_sem.at[nth], mate)
        copy.start()
        l_copy[nth] = copy

    def level_two(j, nth):
        if nth == 0:
            u2_copy.wait_recv()
        l_copy[nth].wait_recv()
        lanes = pl.ds(j * W, W)
        for g in range(G):
            rhs2[g, 0] = mixed(lown[nth, g])
            rhs2[g, 1] = mixed(lmr[nth, g])
        subs = wedge // sb2

        def block(e, d, start):
            base = (((c + e) % C) * Y + (y + d) % Y) * wedge + start
            rows = pl.ds(pl.multiple_of(base, sb2), sb2)
            re = im = 0.0
            for g in range(G):
                values = dot(u2[k, g, rows, :], rhs2[g, 0]) + dot(u2m[g, rows, :], rhs2[g, 1])
                r, i = turned(values, ph2[g, rows, lanes])
                re = re + r
                im = im + i
            return re, im

        for e in range(1, C):

            @pl.loop(0, Y * subs)
            def _(t):
                d = t // subs
                start = (t % subs) * sb2
                rows = pl.ds(pl.multiple_of(start, sb2), sb2)
                re, im = block(e, d, start)
                xsnd[nth, e - 1, d, rows, :W] = re.astype(jnp.bfloat16)
                xsnd[nth, e - 1, d, rows, W:] = im.astype(jnp.bfloat16)

            copy = remote(xsnd.at[nth, e - 1], xrcv.at[nth, e - 1], x_sem.at[nth, e - 1], x_peer(e))
            copy.start()
            x_copy[nth, e] = copy

        @pl.loop(0, Y * subs)
        def _(t):
            d = t // subs
            start = (t % subs) * sb2
            rows = pl.ds(pl.multiple_of(start, sb2), sb2)
            re, im = block(0, d, start)
            iown[nth, d, rows, :W] = re
            iown[nth, d, rows, W:] = im

    def sum_x(nth):
        for e in range(1, C):
            x_copy[nth, e].wait_recv()
        for d in range(1, Y):
            total = iown[nth, d]
            for e in range(1, C):
                total = total + xrcv[nth, e - 1, d].astype(jnp.float32)
            y2s[nth, d - 1] = total.astype(jnp.bfloat16)
            copy = remote(y2s.at[nth, d - 1], y2r.at[nth, d - 1], y2_sem.at[nth, d - 1], y_peer(d))
            copy.start()
            y2_copy[nth, d] = copy

    def finish(j, nth):
        for d in range(1, Y):
            y2_copy[nth, d].wait_recv()
        total = iown[nth, 0]
        for e in range(1, C):
            total = total + xrcv[nth, e - 1, 0].astype(jnp.float32)
        for d in range(1, Y):
            total = total + y2r[nth, d - 1].astype(jnp.float32)
        out[:, j * W : (j + 1) * W] = total[:, :W]
        out[:, R + j * W : R + (j + 1) * W] = total[:, W:]

    order = list(range(1, NB - 1)) + [0, NB - 1]
    for t in range(NB + 5):
        if 0 <= t - 5 < NB:
            finish(order[t - 5], t - 5)
        if 0 <= t - 4 < NB:
            sum_x(t - 4)
        if 0 <= t - 2 < NB:
            sum_y(t - 2)
        if 0 <= t - 1 < NB:
            sum_cores(t - 1)
        if 0 <= t - 3 < NB:
            level_two(order[t - 3], t - 3)
        if t < NB:
            if order[t] == 0:
                fill_halo()
            level_one(order[t], t)

    for group in (core_copy, y_copy, l_copy, x_copy, y2_copy):
        sent.extend(group.values())
    for copy in sent:
        copy.wait_send()

    @pl.when(z < Z - 1)
    def _():
        right.wait_send()

    @pl.when(z > 0)
    def _():
        left.wait_send()


def shards(echoes, exponents, replica, interp0, upsample1, phase1, upsample2, phase2):
    S, L, _, R = echoes.shape
    G = upsample2.shape[0]
    B0 = interp0.shape[3]
    B1 = upsample1.shape[3]
    B2 = upsample2.shape[3]
    C, F, Z = lax.axis_size("coarse"), lax.axis_size("fine"), lax.axis_size("swath")
    Y = F // 2
    K = S // G
    nb = B1 // F
    wedge = B2 // (C * F)
    W = CHUNK
    NB = R // W
    taps_count = replica.shape[1]
    half = (taps_count - 1) // 2
    bf16, f32 = jnp.bfloat16, jnp.float32

    factors = jnp.repeat(jnp.exp2(exponents.astype(f32) - 8.0), R // exponents.shape[2], axis=2)
    samples = (echoes.astype(f32) * factors[:, :, None, :]).astype(bf16)
    samples = samples.transpose(2, 0, 1, 3).reshape(2, S * L, R)
    width = 4 * W
    line = replica.astype(f32)
    taps = jnp.concatenate([line[:, :1], jnp.zeros((2, width - taps_count), f32), line[:, :0:-1]], axis=1)
    w0 = interp0.transpose(1, 3, 0, 2).reshape(S, B0, 2 * L)
    w1 = upsample1.transpose(1, 3, 0, 2).reshape(S, B1, 2 * B0)
    ph1 = phase1.transpose(1, 0, 2)
    u2 = upsample2.reshape(G, 2, nb, C * Y, 2, wedge).transpose(4, 0, 3, 5, 1, 2).reshape(2, G, C * Y * wedge, 2 * nb)
    core = lax.axis_index("fine") % 2
    ph2 = lax.dynamic_index_in_dim(phase2.reshape(C * Y, 2, wedge, G, R), core, 1, keepdims=False)
    ph2 = ph2.reshape(C * Y * wedge, G, R).transpose(1, 0, 2)

    dims = (C, Y, Z, G, K, S, L, B0, nb, wedge, NB, half)
    dma = pltpu.SemaphoreType.DMA
    vm = pltpu.VMEM
    spec = pl.BlockSpec(memory_space=pltpu.VMEM)
    flat = pl.pallas_call(
        functools.partial(kernel, dims),
        out_shape=jax.ShapeDtypeStruct((wedge, 2 * R), f32),
        in_specs=[spec] * 7,
        out_specs=spec,
        scratch_shapes=[
            vm((2, S * L, R + 2 * W), bf16),
            vm((2, S * L, W), bf16),
            vm((2, S * L, W), bf16),
            vm((2, 3 * W, 2 * W), bf16),
            vm((S, 2 * B0, 2 * W), bf16),
            vm((G, 2, 2 * nb, 2 * W), bf16),
            vm((G, C * Y * wedge, 2 * nb), bf16),
            vm((NB, Y, G, nb, 2 * W), f32),
            vm((NB, Y, G, nb, 2 * W), bf16),
            vm((NB, Y, G, nb, 2 * W), bf16),
            vm((NB, Y - 1, G, nb, 2 * W), bf16),
            vm((NB, Y - 1, G, nb, 2 * W), bf16),
            vm((NB, G, nb, 2 * W), bf16),
            vm((NB, G, nb, 2 * W), bf16),
            vm((NB, C - 1, Y, wedge, 2 * W), bf16),
            vm((NB, C - 1, Y, wedge, 2 * W), bf16),
            vm((NB, Y, wedge, 2 * W), f32),
            vm((NB, Y - 1, wedge, 2 * W), bf16),
            vm((NB, Y - 1, wedge, 2 * W), bf16),
            dma((2,)),
            dma((2, 2)),
            dma((NB, 2)),
            dma((NB, Y - 1, 2)),
            dma((NB, 2)),
            dma((NB, C - 1, 2)),
            dma((NB, Y - 1, 2)),
        ],
        compiler_params=pltpu.CompilerParams(
            collective_id=0, has_side_effects=True, vmem_limit_bytes=48 * 1024 * 1024
        ),
    )(samples, taps, w0, w1, ph1, u2, ph2)
    return flat.reshape(wedge, 2, R)


def solution(mesh):
    in_specs = (
        P(("coarse", "fine"), None, None, "swath"),
        P(("coarse", "fine"), None, "swath"),
        P(),
        P(None, ("coarse", "fine"), None, None),
        P(None, ("coarse", "fine"), None, None),
        P(None, ("coarse", "fine"), "swath"),
        P("coarse", None, "fine", None),
        P(None, "coarse", "swath"),
    )
    out_specs = P(("coarse", "fine"), None, "swath")
    return jax.shard_map(shards, mesh=mesh, in_specs=in_specs, out_specs=out_specs, check_vma=False)
```

time: 244 us -> 83.8 us (0.34)
  waiting for transfers between devices: 117 us -> 0 us
  Pallas kernels: 0 us -> 54.2 us
  other arithmetic: 40.8 us -> 0.57 us
  local copies, waits for them, and re-layouts: 47.8 us -> 28.3 us
  between operations: 14.2 us -> 0.13 us
  matrix products: 12 us -> 0 us
  starting transfers between devices: 10.7 us -> 0 us
    unnamed x4 -> x0, waiting for transfers between devices: 61.3 us -> none
    pallas_call x0 -> x1, Pallas kernels: none -> 54.2 us  [shards(): pl.pallas_call(functools.partial(kernel, dims), out_shape=jax.ShapeDtypeS...]
    reduce_scatter x1 -> x0, waiting for transfers between devices: 46.9 us -> none  [shards(): lax.psum_scatter(jnp.sum(rotated.reshape(lax.axis_size('fine') * local_ro...]
    sub x2 -> x0, other arithmetic: 16.5 us -> none  [rotate(): real_out = cosine * values[:, 0] - sine * values[:, 1]]
    dot_general x7 -> x0, matrix products: 12 us -> none  [the longest x1 4.7 us: second_term(): jnp.einsum('gibon,bigr->nogr', mixer, children, preferred_element_type=jn...]
    unnamed x41 -> x21, local copies, waits for them, and re-layouts: 15.6 us -> 6.32 us
    all_to_all x1 -> x0, waiting for transfers between devices: 9.09 us -> none  [shards(): lax.all_to_all(shaped, 'fine', split_axis=4, concat_axis=2, tiled=True)]
    sin x1 -> x0, other arithmetic: 8.3 us -> none  [rotate(): sine = jnp.sin(radians)]
  transfers between devices with their start and end apart: 6 -> 0, of which waited for: 3 -> 0; matrix products, arithmetic and copies ran while one was open for 20% -> 0% of each run, Pallas kernels for 0% -> 0%
where the time goes in v1:
time: 83.8 us; the launch traced here: 83.2 us
  Pallas kernels  54.2 us (65%)
  local copies, waits for them, and re-layouts  28.3 us (34%)
    pallas_call x1, Pallas kernels, shards(): pl.pallas_call(functools.partial(kernel, dims), out_shape=jax.ShapeDtypeS...  54.2 us
    reshape x3, local copies, waits for them, and re-layouts, shards(): upsample2.reshape(G, 2, nb, C * Y, 2, wedge).transpose(4, 0, 3, 5, 1, 2)  14.3 us
    unnamed x21, local copies, waits for them, and re-layouts  6.32 us
    dynamic_slice x1, local copies, waits for them, and re-layouts, shards(): lax.dynamic_index_in_dim(phase2.reshape(C * Y, 2, wedge, G, R), core, 1,...  3.03 us
    reshape x1, local copies, waits for them, and re-layouts, shards(): return flat.reshape(wedge, 2, R)  1.86 us

profile of v1, /device:TPU:0, one launch (start us, length us, event | category | flops | bytes accessed | tf_op | source)
XLA Modules:
  0.0 83.2 jit_solution(13387308748076647450)
XLA Ops:
  0.0 3.0 %constant_dynamic-slice_fusion = bf16[4,1,256,2,512]{4,3,2,1,0:T(2,128)(2,1)S(1)} fusion(bf16[4,2,256,2,512]{4,3,2,1,0:T(2,128)(2,1)} %bitcast.24, s32[]{:T(128)S(6)} %select_n.12), kind=kLoop, calls=%fused_computation.5 | loop fusion | bytes 4194308 | tf_op jit(solution)/shard_map/jit(dynamic_index_in_dim)/dynamic_slice | solution.py:328
  3.0 0.0 copy-start.2
  3.0 1.7 %copy.24 = bf16[4,1,256,2,512]{4,2,0,3,1:T(8,128)(2,1)} copy(bf16[4,1,256,2,512]{4,3,2,1,0:T(2,128)(2,1)S(1)} %constant_dynamic-slice_fusion) | data formatting | bytes 4194304
  4.8 0.5 copy-done.2
  5.2 2.8 %reshape.29 = bf16[2,2,128,4,2,256]{5,4,3,2,1,0:T(2,128)(2,1)} reshape(bf16[2,2,128,2048]{3,2,1,0:T(8,128)(2,1)S(1)} %copy-done.2) | data formatting | bytes 4194304 | tf_op jit(solution)/shard_map/reshape | solution.py:326
  8.0 9.0 %copy.21 = bf16[2,2,128,4,2,256]{2,1,5,3,0,4:T(2,128)(2,1)S(1)} copy(bf16[2,2,128,4,2,256]{5,4,3,2,1,0:T(2,128)(2,1)} %reshape.29) | data formatting | bytes 4194304 | tf_op jit(solution)/shard_map/reshape | solution.py:326
  16.9 0.0 copy-start.7
  17.0 2.6 %reshape.30.u2 = bf16[2,2,1024,256]{3,2,1,0:T(8,128)(2,1)} reshape(bf16[2,2,4,256,2,128]{5,4,3,2,1,0:T(2,128)(2,1)S(1)} %bitcast.20) | data formatting | bytes 4194304 | tf_op jit(solution)/shard_map/reshape | solution.py:326
  19.6 0.0 copy-done.7
  19.6 0.0 copy-start.4
  19.6 0.1 broadcast_in_dim.6
  19.7 0.3 copy.16
  20.0 0.8 copy-done.4
  20.8 0.0 copy-start.3
  20.8 0.5 fusion
  21.4 0.9 %copy.17 = bf16[2,4,64,512]{3,2,1,0:T(8,128)(2,1)} copy(bf16[2,4,64,512]{3,0,2,1:T(2,128)(2,1)S(1)} %fusion) | data formatting | bytes 1048576 | tf_op jit(solution)/shard_map/transpose | solution.py:319
  22.2 0.2 copy-done.3
  22.4 0.0 copy-start.5
  22.4 0.4 copy.26
  22.8 0.0 copy-start.6
  22.8 0.0 copy-start.8
  22.8 0.6 copy-done.5
  23.5 1.0 %copy.23.w1 = bf16[4,512,128]{2,1,0:T(8,128)(2,1)} copy(bf16[4,512,128]{1,2,0:T(8,128)(2,1)S(1)} %bitcast.23) | data formatting | bytes 1048576 | tf_op jit(solution)/shard_map/reshape | solution.py:324
  24.5 0.0 copy-done.6
  24.5 0.1 copy.18
  24.7 0.1 reshape.27.w0
  24.8 0.1 pad.1.clone
  24.9 0.0 copy-done.8
  24.9 0.1 slice.9
  24.9 0.1 rev.3
  25.0 0.0 copy-start
  25.1 1.0 %copy-done = bf16[2,4,64,512]{3,2,1,0:T(8,128)(2,1)S(1)} copy-done((bf16[2,4,64,512]{3,2,1,0:T(8,128)(2,1)S(1)}, bf16[2,4,64,512]{3,2,1,0:T(8,128)(2,1)}, u32[]{:S(2)}) %copy-start) | copy-done | bytes 524312
  26.1 0.0 copy-start.1
  26.1 1.0 %copy-done.1 = bf16[4,512,128]{2,1,0:T(8,128)(2,1)S(1)} copy-done((bf16[4,512,128]{2,1,0:T(8,128)(2,1)S(1)}, bf16[4,512,128]{2,1,0:T(8,128)(2,1)}, u32[]{:S(2)}) %copy-start.1) | copy-done | bytes 524312
  27.1 54.2 %shard_map.82 = f32[256,1024]{1,0:T(8,128)S(1)} custom-call(bf16[2,256,512]{2,1,0:T(8,128)(2,1)S(1)} %bitcast.19, f32[2,512]{1,0:T(2,128)S(1)} %pad_maximum_fusion.taps, bf16[4,64,128]{2,1,0:T(8,128)(2,1)S(1)} %reshape.27.w0, bf16[4,512,128]{2,1,0:T(8,128)(2,1)S(1)} %copy-done.1, bf16[4,512,512]{2,1,0:T(8,128)(2,1)S(1)} %bitcast.18, ...), custom_call_target="tpu_custom_call" | custom-call | tf_op jit(solution)/shard_map/pallas_call | solution.py:335
  81.4 1.9 %reshape.33 = f32[256,2,512]{2,1,0:T(2,128)} reshape(f32[256,1024]{1,0:T(8,128)S(1)} %shard_map.82) | data formatting | bytes 2097152 | tf_op jit(solution)/shard_map/reshape | solution.py:372
  (5 shorter events, 0.1 us)
Async XLA Ops:
  3.0 2.2 %copy-start.2 = (bf16[2,2,128,2048]{3,2,1,0:T(8,128)(2,1)S(1)}, bf16[2,2,128,2048]{3,2,1,0:T(8,128)(2,1)}, u32[]{:S(2)}) copy-start(bf16[2,2,128,2048]{3,2,1,0:T(8,128)(2,1)} %param.14) | copy-start | bytes 6291460
  16.9 2.6 %copy-start.7 = (s32[4,64,16]{1,2,0:T(8,128)S(1)}, s32[4,64,16]{1,2,0:T(8,128)}, u32[]{:S(2)}) copy-start(s32[4,64,16]{1,2,0:T(8,128)} %param.9) | copy-start | bytes 49156
  19.6 1.2 %copy-start.4 = (s32[4,64,2,512]{3,2,1,0:T(2,128)S(1)}, s32[4,64,2,512]{3,2,1,0:T(2,128)}, u32[]{:S(2)}) copy-start(s32[4,64,2,512]{3,2,1,0:T(2,128)} %param.8) | copy-start | bytes 3145732
  20.8 1.6 %copy-start.3 = (bf16[512,4,512]{2,1,0:T(4,128)(2,1)S(1)}, bf16[512,4,512]{2,1,0:T(4,128)(2,1)}, u32[]{:S(2)}) copy-start(bf16[512,4,512]{2,1,0:T(4,128)(2,1)} %param.13) | copy-start | bytes 6291460
  22.4 1.0 %copy-start.5 = (bf16[2,4,64,512]{3,2,1,0:T(8,128)(2,1)S(1)}, bf16[2,4,64,512]{3,2,1,0:T(8,128)(2,1)}, u32[]{:S(2)}) copy-start(bf16[2,4,64,512]{3,2,1,0:T(8,128)(2,1)} %param.12) | copy-start | bytes 1572868
  22.8 1.7 %copy-start.6 = (bf16[2,4,64,64]{3,2,1,0:T(8,128)(2,1)S(1)}, bf16[2,4,64,64]{3,2,1,0:T(8,128)(2,1)}, u32[]{:S(2)}) copy-start(bf16[2,4,64,64]{3,2,1,0:T(8,128)(2,1)} %param.11) | copy-start | bytes 196612
  22.8 2.0 %copy-start.8 = (bf16[2,129]{1,0:T(2,128)(2,1)S(1)}, bf16[2,129]{1,0:T(2,128)(2,1)}, u32[]{:S(2)}) copy-start(bf16[2,129]{1,0:T(2,128)(2,1)} %param.10) | copy-start | bytes 1552
  25.0 1.0 %copy-start = (bf16[2,4,64,512]{3,2,1,0:T(8,128)(2,1)S(1)}, bf16[2,4,64,512]{3,2,1,0:T(8,128)(2,1)}, u32[]{:S(2)}) copy-start(bf16[2,4,64,512]{3,2,1,0:T(8,128)(2,1)} %copy.17) | copy-start | bytes 1572868
  26.1 1.0 %copy-start.1 = (bf16[4,512,128]{2,1,0:T(8,128)(2,1)S(1)}, bf16[4,512,128]{2,1,0:T(8,128)(2,1)}, u32[]{:S(2)}) copy-start(bf16[4,512,128]{2,1,0:T(8,128)(2,1)} %copy.23.w1) | copy-start | bytes 1572868

commit v2 on v1

--- a/solution.py
+++ b/solution.py
@@ -47,8 +47,8 @@
 
 
 def kernel(
-    dims, samples, taps, w0, w1, ph1, u2, ph2, out,
-    xs, halo_l, halo_r, band, rhs1, rhs2, u2m, pown, pms, pmr, ys, yr, lown, lmr, xsnd, xrcv, iown, y2s, y2r,
+    dims, samples, taps, interp0, upsample1, ph1, u2, ph2, out,
+    w0, w1, u2t, xs, halo_l, halo_r, band, rhs1, rhs2, u2m, pown, pms, pmr, ys, yr, lown, lmr, xsnd, xrcv, iown, y2s, y2r,
     u2_sem, halo_sem, core_sem, y_sem, l_sem, x_sem, y2_sem,
 ):
     C, Y, Z, G, K, S, L, B0, nb, wedge, NB, half = dims
@@ -99,9 +99,9 @@
     def _():
         left.start()
 
-    u2_copy = remote(u2.at[1 - k], u2m, u2_sem, mate)
-    u2_copy.start()
-    sent = [u2_copy]
+    for s in range(S):
+        w0[s] = jnp.concatenate([interp0[0, s], interp0[1, s]], axis=0).T
+        w1[s] = jnp.concatenate([upsample1[0, s], upsample1[1, s]], axis=0).T
 
     reach = 3 * W
     width = taps.shape[1]
@@ -136,8 +136,18 @@
             xs[:, :, W + R : R + 2 * W] = jnp.zeros((2, S * L, W), jnp.bfloat16)
 
     core_copy, y_copy, l_copy, x_copy, y2_copy = {}, {}, {}, {}, {}
-    sb1 = min(nb, 64)
-    sb2 = min(wedge, 64)
+    u2_copy = remote(u2t.at[:, :, 1 - k], u2m, u2_sem, mate)
+    sub = 64
+
+    def turn_columns():
+        step = max(wedge, W)
+        for g in range(G):
+            for first in range(0, u2.shape[3], step):
+                block = u2[g, :, :, first : first + step].reshape(2 * nb, step).T
+                for i in range(step // wedge):
+                    q = first // wedge + i
+                    u2t[g, q // 2, q % 2] = block[i * wedge : (i + 1) * wedge]
+        u2_copy.start()
 
     def level_one(j, nth):
         lanes = pl.ds(j * W, W)
@@ -146,40 +156,33 @@
         for s in range(S):
             beams = dot(w0[s], mixed(comp[s * L : (s + 1) * L])).astype(jnp.bfloat16)
             rhs1[s] = mixed(beams)
-        subs = nb // sb1
-
-        def block(core, t):
-            d = t // (G * subs)
-            g = (t // subs) % G
-            start = (t % subs) * sb1
-            rows = pl.ds(pl.multiple_of((((y + d) % Y) * 2 + core) * nb + start, sb1), sb1)
-            re = im = 0.0
-            for kid in range(K):
-                s = g * K + kid
-                r, i = turned(dot(w1[s, rows, :], rhs1[s]), ph1[s, rows, lanes])
-                re = re + r
-                im = im + i
-            return d, g, pl.ds(pl.multiple_of(start, sb1), sb1), re, im
-
-        @pl.loop(0, Y * G * subs)
-        def _(t):
-            d, g, rows, re, im = block(1 - k, t)
-            pms[nth, d, g, rows, :W] = re.astype(jnp.bfloat16)
-            pms[nth, d, g, rows, W:] = im.astype(jnp.bfloat16)
-
-        copy = remote(pms.at[nth], pmr.at[nth], core_sem.at[nth], mate)
-        copy.start()
-        core_copy[nth] = copy
-
-        @pl.loop(0, Y * G * subs)
-        def _(t):
-            d, g, rows, re, im = block(k, t)
-            pown[nth, d, g, rows, :W] = re
-            pown[nth, d, g, rows, W:] = im
+        def block(core, d, store):
+            base = pl.multiple_of((((y + d) % Y) * 2 + core) * nb, nb)
+            for g in range(G):
+                values = [dot(w1[g * K + kid, pl.ds(base, nb), :], rhs1[g * K + kid]) for kid in range(K)]
+                for start in range(0, nb, sub):
+                    size = min(sub, nb - start)
+                    rows = pl.ds(pl.multiple_of(base + start, size), size)
+                    re = im = 0.0
+                    for kid in range(K):
+                        r, i = turned(values[kid][start : start + size], ph1[g * K + kid, rows, lanes])
+                        re = re + r
+                        im = im + i
+                    store[g, start : start + size, :W] = re.astype(store.dtype)
+                    store[g, start : start + size, W:] = im.astype(store.dtype)
+
+        offsets = list(range(1, Y)) + [0]
+        for d in offsets:
+            block(1 - k, d, pms.at[nth, d])
+            copy = remote(pms.at[nth, d], pmr.at[nth, d], core_sem.at[nth, d], mate)
+            copy.start()
+            core_copy[nth, d] = copy
+        for d in offsets:
+            block(k, d, pown.at[nth, d])
 
     def sum_cores(nth):
-        core_copy[nth].wait_recv()
-        for d in range(1, Y):
+        for d in range(1, Y):
+            core_copy[nth, d].wait_recv()
             for g in range(G):
                 ys[nth, d - 1, g] = (pown[nth, d, g] + pmr[nth, d, g].astype(jnp.float32)).astype(jnp.bfloat16)
             copy = remote(ys.at[nth, d - 1], yr.at[nth, d - 1], y_sem.at[nth, d - 1], y_peer(d))
@@ -187,6 +190,7 @@
             y_copy[nth, d] = copy
 
     def sum_y(nth):
+        core_copy[nth, 0].wait_recv()
         for d in range(1, Y):
             y_copy[nth, d].wait_recv()
         for g in range(G):
@@ -204,51 +208,37 @@
         l_copy[nth].wait_recv()
         lanes = pl.ds(j * W, W)
         for g in range(G):
-            rhs2[g, 0] = mixed(lown[nth, g])
-            rhs2[g, 1] = mixed(lmr[nth, g])
-        subs = wedge // sb2
-
-        def block(e, d, start):
-            base = (((c + e) % C) * Y + (y + d) % Y) * wedge + start
-            rows = pl.ds(pl.multiple_of(base, sb2), sb2)
-            re = im = 0.0
-            for g in range(G):
-                values = dot(u2[k, g, rows, :], rhs2[g, 0]) + dot(u2m[g, rows, :], rhs2[g, 1])
-                r, i = turned(values, ph2[g, rows, lanes])
-                re = re + r
-                im = im + i
-            return re, im
-
+            rhs2[g, : 2 * nb] = mixed(lown[nth, g])
+            rhs2[g, 2 * nb :] = mixed(lmr[nth, g])
+
+        def block(e, d, store):
+            q = ((c + e) % C) * Y + (y + d) % Y
+            values = [dot(jnp.concatenate([u2t[g, q, k], u2m[g, q]], axis=1), rhs2[g]) for g in range(G)]
+            for start in range(0, wedge, sub):
+                size = min(sub, wedge - start)
+                re = im = 0.0
+                for g in range(G):
+                    r, i = turned(values[g][start : start + size], ph2[g, q, k, start : start + size, lanes])
+                    re = re + r
+                    im = im + i
+                store[start : start + size, :W] = re.astype(store.dtype)
+                store[start : start + size, W:] = im.astype(store.dtype)
+
+        offsets = list(range(1, Y)) + [0]
         for e in range(1, C):
-
-            @pl.loop(0, Y * subs)
-            def _(t):
-                d = t // subs
-                start = (t % subs) * sb2
-                rows = pl.ds(pl.multiple_of(start, sb2), sb2)
-                re, im = block(e, d, start)
-                xsnd[nth, e - 1, d, rows, :W] = re.astype(jnp.bfloat16)
-                xsnd[nth, e - 1, d, rows, W:] = im.astype(jnp.bfloat16)
-
-            copy = remote(xsnd.at[nth, e - 1], xrcv.at[nth, e - 1], x_sem.at[nth, e - 1], x_peer(e))
-            copy.start()
-            x_copy[nth, e] = copy
-
-        @pl.loop(0, Y * subs)
-        def _(t):
-            d = t // subs
-            start = (t % subs) * sb2
-            rows = pl.ds(pl.multiple_of(start, sb2), sb2)
-            re, im = block(0, d, start)
-            iown[nth, d, rows, :W] = re
-            iown[nth, d, rows, W:] = im
+            for d in offsets:
+                block(e, d, xsnd.at[nth, e - 1, d])
+                copy = remote(xsnd.at[nth, e - 1, d], xrcv.at[nth, e - 1, d], x_sem.at[nth, e - 1, d], x_peer(e))
+                copy.start()
+                x_copy[nth, e, d] = copy
+        for d in offsets:
+            block(0, d, iown.at[nth, d])
 
     def sum_x(nth):
-        for e in range(1, C):
-            x_copy[nth, e].wait_recv()
         for d in range(1, Y):
             total = iown[nth, d]
             for e in range(1, C):
+                x_copy[nth, e, d].wait_recv()
                 total = total + xrcv[nth, e - 1, d].astype(jnp.float32)
             y2s[nth, d - 1] = total.astype(jnp.bfloat16)
             copy = remote(y2s.at[nth, d - 1], y2r.at[nth, d - 1], y2_sem.at[nth, d - 1], y_peer(d))
@@ -260,6 +250,7 @@
             y2_copy[nth, d].wait_recv()
         total = iown[nth, 0]
         for e in range(1, C):
+            x_copy[nth, e, 0].wait_recv()
             total = total + xrcv[nth, e - 1, 0].astype(jnp.float32)
         for d in range(1, Y):
             total = total + y2r[nth, d - 1].astype(jnp.float32)
@@ -268,21 +259,24 @@
 
     order = list(range(1, NB - 1)) + [0, NB - 1]
     for t in range(NB + 5):
-        if 0 <= t - 5 < NB:
-            finish(order[t - 5], t - 5)
-        if 0 <= t - 4 < NB:
-            sum_x(t - 4)
-        if 0 <= t - 2 < NB:
-            sum_y(t - 2)
-        if 0 <= t - 1 < NB:
-            sum_cores(t - 1)
-        if 0 <= t - 3 < NB:
-            level_two(order[t - 3], t - 3)
         if t < NB:
             if order[t] == 0:
                 fill_halo()
             level_one(order[t], t)
-
+        if t == 0:
+            turn_columns()
+        if 0 <= t - 2 < NB:
+            level_two(order[t - 2], t - 2)
+        if t < NB:
+            sum_cores(t)
+        if 0 <= t - 1 < NB:
+            sum_y(t - 1)
+        if 0 <= t - 4 < NB:
+            sum_x(t - 4)
+        if 0 <= t - 5 < NB:
+            finish(order[t - 5], t - 5)
+
+    sent = [u2_copy]
     for group in (core_copy, y_copy, l_copy, x_copy, y2_copy):
         sent.extend(group.values())
     for copy in sent:
@@ -320,13 +314,8 @@
     width = 4 * W
     line = replica.astype(f32)
     taps = jnp.concatenate([line[:, :1], jnp.zeros((2, width - taps_count), f32), line[:, :0:-1]], axis=1)
-    w0 = interp0.transpose(1, 3, 0, 2).reshape(S, B0, 2 * L)
-    w1 = upsample1.transpose(1, 3, 0, 2).reshape(S, B1, 2 * B0)
     ph1 = phase1.transpose(1, 0, 2)
-    u2 = upsample2.reshape(G, 2, nb, C * Y, 2, wedge).transpose(4, 0, 3, 5, 1, 2).reshape(2, G, C * Y * wedge, 2 * nb)
-    core = lax.axis_index("fine") % 2
-    ph2 = lax.dynamic_index_in_dim(phase2.reshape(C * Y, 2, wedge, G, R), core, 1, keepdims=False)
-    ph2 = ph2.reshape(C * Y * wedge, G, R).transpose(1, 0, 2)
+    ph2 = phase2.transpose(1, 0, 2).reshape(G, C * Y, 2, wedge, R)
 
     dims = (C, Y, Z, G, K, S, L, B0, nb, wedge, NB, half)
     dma = pltpu.SemaphoreType.DMA
@@ -338,13 +327,16 @@
         in_specs=[spec] * 7,
         out_specs=spec,
         scratch_shapes=[
+            vm((S, B0, 2 * L), bf16),
+            vm((S, B1, 2 * B0), bf16),
+            vm((G, C * Y, 2, wedge, 2 * nb), bf16),
             vm((2, S * L, R + 2 * W), bf16),
             vm((2, S * L, W), bf16),
             vm((2, S * L, W), bf16),
             vm((2, 3 * W, 2 * W), bf16),
             vm((S, 2 * B0, 2 * W), bf16),
-            vm((G, 2, 2 * nb, 2 * W), bf16),
-            vm((G, C * Y * wedge, 2 * nb), bf16),
+            vm((G, 4 * nb, 2 * W), bf16),
+            vm((G, C * Y, wedge, 2 * nb), bf16),
             vm((NB, Y, G, nb, 2 * W), f32),
             vm((NB, Y, G, nb, 2 * W), bf16),
             vm((NB, Y, G, nb, 2 * W), bf16),
@@ -359,16 +351,16 @@
             vm((NB, Y - 1, wedge, 2 * W), bf16),
             dma((2,)),
             dma((2, 2)),
-            dma((NB, 2)),
+            dma((NB, Y, 2)),
             dma((NB, Y - 1, 2)),
             dma((NB, 2)),
-            dma((NB, C - 1, 2)),
+            dma((NB, C - 1, Y, 2)),
             dma((NB, Y - 1, 2)),
         ],
         compiler_params=pltpu.CompilerParams(
-            collective_id=0, has_side_effects=True, vmem_limit_bytes=48 * 1024 * 1024
+            collective_id=0, has_side_effects=True, vmem_limit_bytes=28 * 1024 * 1024
         ),
-    )(samples, taps, w0, w1, ph1, u2, ph2)
+    )(samples, taps, interp0, upsample1, ph1, upsample2, ph2)
     return flat.reshape(wedge, 2, R)
 
 

time: 83.8 us -> 51.4 us (0.61)
  local copies, waits for them, and re-layouts: 28.3 us -> 8.55 us
  Pallas kernels: 54.2 us -> 39.9 us
  other arithmetic: 0.57 us -> 2.68 us
    reshape x5 -> x0, local copies, waits for them, and re-layouts: 15.5 us -> none  [the longest x3 14.3 us: shards(): upsample2.reshape(G, 2, nb, C * Y, 2, wedge).transpose(4, 0, 3, 5, 1, 2)]
    pallas_call x1, Pallas kernels: 54.2 us -> 39.9 us  [shards(): pl.pallas_call(functools.partial(kernel, dims), out_shape=jax.ShapeDtypeS...]
    unnamed x21 -> x11, local copies, waits for them, and re-layouts: 6.32 us -> 3.2 us
    dynamic_slice x1 -> x0, local copies, waits for them, and re-layouts: 3.03 us -> none  [shards(): lax.dynamic_index_in_dim(phase2.reshape(C * Y, 2, wedge, G, R), core, 1,...]
    transpose x1, other arithmetic: 0.54 us -> 1.9 us  [shards(): samples = samples.transpose(2, 0, 1, 3).reshape(2, S * L, R)]
where the time goes in v2:
time: 51.4 us; the launch traced here: 51.2 us
  Pallas kernels  39.9 us (78%)
  local copies, waits for them, and re-layouts  8.55 us (17%)
  other arithmetic  2.68 us (5%)
    pallas_call x1, Pallas kernels, shards(): pl.pallas_call(functools.partial(kernel, dims), out_shape=jax.ShapeDtypeS...  39.9 us
    unnamed x11, local copies, waits for them, and re-layouts  3.2 us
    transpose x1, other arithmetic, shards(): samples = samples.transpose(2, 0, 1, 3).reshape(2, S * L, R)  1.9 us
    reshape x1, local copies, waits for them, and re-layouts, shards(): return flat.reshape(wedge, 2, R)  1.86 us
    mul x1, local copies, waits for them, and re-layouts, shards(): samples = (echoes.astype(f32) * factors[:, :, None, :]).astype(bf16)  1.11 us

profile of v2, /device:TPU:0, one launch (start us, length us, event | category | flops | bytes accessed | tf_op | source)
XLA Modules:
  0.0 51.2 jit_solution(10074937084732459098)
XLA Ops:
  0.0 0.7 %slice.9 = f32[2,128]{1,0:T(2,128)S(1)} slice(bf16[2,129]{1,0:T(2,128)(2,1)} %param.10), slice={[0:2], [1:129]} | slice | bytes 2048 | tf_op jit(solution)/shard_map/slice | solution.py:316
  0.8 0.1 rev.3
  0.8 0.7 %slice.8 = f32[2,1]{1,0:T(2,128)S(1)} slice(bf16[2,129]{1,0:T(2,128)(2,1)} %param.10), slice={[0:2], [0:1]} | slice | bytes 16 | tf_op jit(solution)/shard_map/slice | solution.py:316
  1.5 0.1 pad.1.clone
  1.6 0.8 %multiply_exponential_fusion = f32[4,64,16]{1,2,0:T(8,128)S(1)} fusion(s32[4,64,16]{1,2,0:T(8,128)} %param.9), kind=kLoop, calls=%fused_computation.3 | loop fusion | flops 12288 | bytes 32768 | tf_op jit(solution)/shard_map/exp2 | solution.py:311
  2.4 0.1 broadcast_in_dim.6
  2.4 0.0 copy-start.4
  2.5 1.1 %copy.13 = f32[4,64,512]{2,1,0:T(8,128)} copy(f32[4,64,512]{1,2,0:T(8,128)S(1)} %bitcast.13) | data formatting | bytes 1048576 | tf_op jit(solution)/shard_map/mul | solution.py:312
  3.6 1.9 %fusion = bf16[2,4,64,512]{3,0,2,1:T(2,128)(2,1)S(1)} fusion(s32[4,64,2,512]{3,2,1,0:T(2,128)} %param.8, f32[4,64,512]{2,1,0:T(8,128)} %copy.13), kind=kLoop, calls=%fused_computation.2 | loop fusion | flops 786432 | bytes 2097152 | tf_op jit(solution)/shard_map/transpose | solution.py:313
  5.5 0.1 copy.14
  5.5 0.0 copy-done.4
  5.5 0.0 copy-start.3
  5.6 0.4 copy.18
  6.0 1.8 %copy-done.3 = bf16[2048,2,512]{2,1,0:T(2,128)(2,1)S(1)} copy-done((bf16[2048,2,512]{2,1,0:T(2,128)(2,1)S(1)}, bf16[2048,2,512]{2,1,0:T(2,128)(2,1)}, u32[]{:S(2)}) %copy-start.3) | copy-done | bytes 4194328
  7.7 0.0 copy-start
  7.7 0.0 copy-start.1
  7.7 0.0 copy-start.2
  7.7 0.7 %copy.16 = bf16[2,2048,512]{2,1,0:T(8,128)(2,1)S(1)} copy(bf16[2,2048,512]{2,0,1:T(2,128)(2,1)S(1)} %bitcast.12) | data formatting | bytes 8388608 | tf_op jit(solution)/shard_map/transpose | solution.py:318
  8.4 0.9 %copy-done = bf16[2,2,128,2048]{3,2,1,0:T(8,128)(2,1)S(1)} copy-done((bf16[2,2,128,2048]{3,2,1,0:T(8,128)(2,1)S(1)}, bf16[2,2,128,2048]{3,2,1,0:T(8,128)(2,1)}, u32[]{:S(2)}) %copy-start) | copy-done | bytes 2097176
  9.3 0.1 copy-done.1
  9.4 0.0 copy-done.2
  9.4 39.9 %shard_map.82 = f32[256,1024]{1,0:T(8,128)S(1)} custom-call(bf16[2,256,512]{2,1,0:T(8,128)(2,1)S(1)} %bitcast.11, f32[2,512]{1,0:T(2,128)S(1)} %pad_maximum_fusion.taps, bf16[2,4,64,64]{3,2,1,0:T(8,128)(2,1)S(1)} %copy-done.2, bf16[2,4,64,512]{3,2,1,0:T(8,128)(2,1)S(1)} %copy-done.1, bf16[4,512,512]{2,1,0:T(8,128)(2,1)S(1)} %bitcast.10, ...), custom_call_target="tpu_custom_call" | custom-call | tf_op jit(solution)/shard_map/pallas_call | solution.py:324
  49.3 1.9 %reshape.12 = f32[256,2,512]{2,1,0:T(2,128)} reshape(f32[256,1024]{1,0:T(8,128)S(1)} %shard_map.82) | data formatting | bytes 2097152 | tf_op jit(solution)/shard_map/reshape | solution.py:364
  (2 shorter events, 0.0 us)
Async XLA Ops:
  2.4 3.1 %copy-start.4 = (bf16[512,4,512]{2,1,0:T(4,128)(2,1)S(1)}, bf16[512,4,512]{2,1,0:T(4,128)(2,1)}, u32[]{:S(2)}) copy-start(bf16[512,4,512]{2,1,0:T(4,128)(2,1)} %param.13) | copy-start | bytes 6291460
  5.5 2.2 %copy-start.3 = (bf16[2048,2,512]{2,1,0:T(2,128)(2,1)S(1)}, bf16[2048,2,512]{2,1,0:T(2,128)(2,1)}, u32[]{:S(2)}) copy-start(bf16[2048,2,512]{2,1,0:T(2,128)(2,1)} %param.15) | copy-start | bytes 12582916
  7.7 1.6 %copy-start = (bf16[2,2,128,2048]{3,2,1,0:T(8,128)(2,1)S(1)}, bf16[2,2,128,2048]{3,2,1,0:T(8,128)(2,1)}, u32[]{:S(2)}) copy-start(bf16[2,2,128,2048]{3,2,1,0:T(8,128)(2,1)} %u2_.1) | copy-start | bytes 6291460
  7.7 1.7 %copy-start.1 = (bf16[2,4,64,512]{3,2,1,0:T(8,128)(2,1)S(1)}, bf16[2,4,64,512]{3,2,1,0:T(8,128)(2,1)}, u32[]{:S(2)}) copy-start(bf16[2,4,64,512]{3,2,1,0:T(8,128)(2,1)} %upsample1.1) | copy-start | bytes 1572868
  7.7 1.7 %copy-start.2 = (bf16[2,4,64,64]{3,2,1,0:T(8,128)(2,1)S(1)}, bf16[2,4,64,64]{3,2,1,0:T(8,128)(2,1)}, u32[]{:S(2)}) copy-start(bf16[2,4,64,64]{3,2,1,0:T(8,128)(2,1)} %interp0.1) | copy-start | bytes 196612

commit v3 on v2

--- a/solution.py
+++ b/solution.py
@@ -47,9 +47,9 @@
 
 
 def kernel(
-    dims, samples, taps, interp0, upsample1, ph1, u2, ph2, out,
-    w0, w1, u2t, xs, halo_l, halo_r, band, rhs1, rhs2, u2m, pown, pms, pmr, ys, yr, lown, lmr, xsnd, xrcv, iown, y2s, y2r,
-    u2_sem, halo_sem, core_sem, y_sem, l_sem, x_sem, y2_sem,
+    dims, echoes, exponents, replica, interp0, upsample1, ph1, u2_hbm, ph2, out,
+    hp, u2, w0, w1, u2t, xs, halo_l, halo_r, band, rhs1, rhs2, u2m, pown, pms, pmr, ys, yr, lown, lmr, xsnd, xrcv, iown, y2s, y2r,
+    load_sem, u2_sem, halo_sem, core_sem, y_sem, l_sem, x_sem, y2_sem,
 ):
     C, Y, Z, G, K, S, L, B0, nb, wedge, NB, half = dims
     W = CHUNK
@@ -67,6 +67,9 @@
     def x_peer(e):
         return {"coarse": (c + e) % C}
 
+    load = pltpu.make_async_copy(u2_hbm, u2, load_sem.at[0])
+    load.start()
+
     barrier = pltpu.get_barrier_semaphore()
     partners = [mate] + [y_peer(d) for d in range(1, Y)] + [x_peer(e) for e in range(1, C)]
     for who in partners:
@@ -80,6 +83,16 @@
     def _():
         pl.semaphore_signal(barrier, inc=1, device_id={"swath": z - 1}, device_id_type=MESH)
 
+    blocks = exponents.shape[1]
+    spread = lax.broadcasted_iota(jnp.int32, (blocks, R), 1) // (R // blocks)
+    spread = (spread == lax.broadcasted_iota(jnp.int32, (blocks, R), 0)).astype(jnp.bfloat16)
+    for s in range(S):
+        powers = jnp.left_shift(jnp.ones_like(exponents[s]), exponents[s]).astype(jnp.float32) * 2.0**-8
+        factors = dot(powers.T.astype(jnp.bfloat16), spread)
+        for part in range(2):
+            values = echoes[s, :, part, :].astype(jnp.float32) * factors
+            xs[part, s * L : (s + 1) * L, W : W + R] = values.astype(jnp.bfloat16)
+
     ends = jnp.where(z > 0, 1, 0) + jnp.where(z < Z - 1, 1, 0)
     pl.semaphore_wait(barrier, len(partners) + ends)
 
@@ -88,8 +101,8 @@
             src_ref=src, dst_ref=dst, send_sem=sems.at[0], recv_sem=sems.at[1], device_id=who, device_id_type=MESH
         )
 
-    right = remote(samples.at[:, :, R - W : R], halo_l, halo_sem.at[0], {"swath": jnp.minimum(z + 1, Z - 1)})
-    left = remote(samples.at[:, :, 0:W], halo_r, halo_sem.at[1], {"swath": jnp.maximum(z - 1, 0)})
+    right = remote(xs.at[:, :, pl.ds(R, W)], halo_l, halo_sem.at[0], {"swath": jnp.minimum(z + 1, Z - 1)})
+    left = remote(xs.at[:, :, pl.ds(W, W)], halo_r, halo_sem.at[1], {"swath": jnp.maximum(z - 1, 0)})
 
     @pl.when(z < Z - 1)
     def _():
@@ -104,17 +117,17 @@
         w1[s] = jnp.concatenate([upsample1[0, s], upsample1[1, s]], axis=0).T
 
     reach = 3 * W
-    width = taps.shape[1]
+    hp[...] = jnp.zeros_like(hp)
+    hp[:, : replica.shape[1]] = replica[...].astype(jnp.float32)
     toeplitz = []
     for part in range(2):
-        row = jnp.broadcast_to(taps[part : part + 1, :], (reach, width))
-        rolled = pltpu.roll(row, (half - W) % width, 1, stride=1, stride_axis=0)
-        toeplitz.append(rolled[:, :W].astype(jnp.bfloat16))
+        row = jnp.broadcast_to(hp[part : part + 1, :], (W, reach))
+        rolled = pltpu.roll(row, W - half, 1, stride=1, stride_axis=0)
+        toeplitz.append(rolled.T.astype(jnp.bfloat16))
     band[0, :, :W] = toeplitz[0]
     band[0, :, W:] = -toeplitz[1]
     band[1, :, :W] = toeplitz[1]
     band[1, :, W:] = toeplitz[0]
-    xs[:, :, W : W + R] = samples[...]
 
     def fill_halo():
         @pl.when(z > 0)
@@ -140,6 +153,7 @@
     sub = 64
 
     def turn_columns():
+        load.wait()
         step = max(wedge, W)
         for g in range(G):
             for first in range(0, u2.shape[3], step):
@@ -258,23 +272,23 @@
         out[:, R + j * W : R + (j + 1) * W] = total[:, W:]
 
     order = list(range(1, NB - 1)) + [0, NB - 1]
-    for t in range(NB + 5):
+    for t in range(NB + 4):
         if t < NB:
             if order[t] == 0:
                 fill_halo()
             level_one(order[t], t)
         if t == 0:
             turn_columns()
-        if 0 <= t - 2 < NB:
-            level_two(order[t - 2], t - 2)
+        if 0 <= t - 1 < NB:
+            sum_y(t - 1)
         if t < NB:
             sum_cores(t)
         if 0 <= t - 1 < NB:
-            sum_y(t - 1)
+            level_two(order[t - 1], t - 1)
+        if 0 <= t - 3 < NB:
+            sum_x(t - 3)
         if 0 <= t - 4 < NB:
-            sum_x(t - 4)
-        if 0 <= t - 5 < NB:
-            finish(order[t - 5], t - 5)
+            finish(order[t - 4], t - 4)
 
     sent = [u2_copy]
     for group in (core_copy, y_copy, l_copy, x_copy, y2_copy):
@@ -304,16 +318,9 @@
     wedge = B2 // (C * F)
     W = CHUNK
     NB = R // W
-    taps_count = replica.shape[1]
-    half = (taps_count - 1) // 2
+    half = (replica.shape[1] - 1) // 2
     bf16, f32 = jnp.bfloat16, jnp.float32
 
-    factors = jnp.repeat(jnp.exp2(exponents.astype(f32) - 8.0), R // exponents.shape[2], axis=2)
-    samples = (echoes.astype(f32) * factors[:, :, None, :]).astype(bf16)
-    samples = samples.transpose(2, 0, 1, 3).reshape(2, S * L, R)
-    width = 4 * W
-    line = replica.astype(f32)
-    taps = jnp.concatenate([line[:, :1], jnp.zeros((2, width - taps_count), f32), line[:, :0:-1]], axis=1)
     ph1 = phase1.transpose(1, 0, 2)
     ph2 = phase2.transpose(1, 0, 2).reshape(G, C * Y, 2, wedge, R)
 
@@ -324,9 +331,11 @@
     flat = pl.pallas_call(
         functools.partial(kernel, dims),
         out_shape=jax.ShapeDtypeStruct((wedge, 2 * R), f32),
-        in_specs=[spec] * 7,
+        in_specs=[spec] * 6 + [pl.BlockSpec(memory_space=pl.ANY), spec],
         out_specs=spec,
         scratch_shapes=[
+            vm((2, 3 * W), f32),
+            vm(upsample2.shape, bf16),
             vm((S, B0, 2 * L), bf16),
             vm((S, B1, 2 * B0), bf16),
             vm((G, C * Y, 2, wedge, 2 * nb), bf16),
@@ -349,6 +358,7 @@
             vm((NB, Y, wedge, 2 * W), f32),
             vm((NB, Y - 1, wedge, 2 * W), bf16),
             vm((NB, Y - 1, wedge, 2 * W), bf16),
+            dma((1,)),
             dma((2,)),
             dma((2, 2)),
             dma((NB, Y, 2)),
@@ -360,7 +370,7 @@
         compiler_params=pltpu.CompilerParams(
             collective_id=0, has_side_effects=True, vmem_limit_bytes=28 * 1024 * 1024
         ),
-    )(samples, taps, interp0, upsample1, ph1, upsample2, ph2)
+    )(echoes, exponents.transpose(0, 2, 1), replica, interp0, upsample1, ph1, upsample2, ph2)
     return flat.reshape(wedge, 2, R)
 
 

time: 51.4 us -> 45.7 us (0.89)
  other arithmetic: 2.68 us -> 0 us
  local copies, waits for them, and re-layouts: 8.55 us -> 6.65 us
  Pallas kernels: 39.9 us -> 38.9 us
    transpose x1 -> x0, other arithmetic: 1.9 us -> none  [shards(): samples = samples.transpose(2, 0, 1, 3).reshape(2, S * L, R)]
    slice x2 -> x0, local copies, waits for them, and re-layouts: 1.41 us -> none  [the longest x1 0.75 us: shards(): line[:, :0:-1]]
    mul x1 -> x0, local copies, waits for them, and re-layouts: 1.11 us -> none  [shards(): samples = (echoes.astype(f32) * factors[:, :, None, :]).astype(bf16)]
    pallas_call x1, Pallas kernels: 39.9 us -> 38.9 us  [shards(): pl.pallas_call(functools.partial(kernel, dims), out_shape=jax.ShapeDtypeS...]
    unnamed x11 -> x15, local copies, waits for them, and re-layouts: 3.2 us -> 4.12 us
    exp2 x1 -> x0, other arithmetic: 0.77 us -> none  [shards(): jnp.exp2(exponents.astype(f32) - 8.0)]
where the time goes in v3:
time: 45.7 us; the launch traced here: 45.6 us
  Pallas kernels  38.9 us (85%)
  local copies, waits for them, and re-layouts  6.65 us (15%)
    pallas_call x1, Pallas kernels, shards(): pl.pallas_call(functools.partial(kernel, dims), out_shape=jax.ShapeDtypeS...  38.9 us
    unnamed x15, local copies, waits for them, and re-layouts  4.12 us
    reshape x1, local copies, waits for them, and re-layouts, shards(): return flat.reshape(wedge, 2, R)  1.86 us

profile of v3, /device:TPU:0, one launch (start us, length us, event | category | flops | bytes accessed | tf_op | source)
XLA Modules:
  0.0 45.6 jit_solution(2364780752190955480)
XLA Ops:
  0.0 0.0 copy-start.6
  0.0 2.1 %copy.12 = bf16[512,4,512]{2,0,1:T(8,128)(2,1)S(1)} copy(bf16[512,4,512]{2,1,0:T(4,128)(2,1)} %param.13) | data formatting | bytes 4194304 | tf_op args[5]
  2.2 0.7 %copy-done.6 = bf16[2048,2,512]{2,1,0:T(2,128)(2,1)S(1)} copy-done((bf16[2048,2,512]{2,1,0:T(2,128)(2,1)S(1)}, bf16[2048,2,512]{2,1,0:T(2,128)(2,1)}, u32[]{:S(2)}) %copy-start.6) | copy-done | bytes 4194328
  2.8 0.0 copy-start
  2.8 0.0 copy-start.1
  2.8 0.0 copy-start.2
  2.8 0.0 copy-start.3
  2.8 0.0 copy-start.4
  2.8 0.0 copy-start.5
  2.9 0.7 %copy.10 = bf16[2,2048,512]{2,1,0:T(8,128)(2,1)S(1)} copy(bf16[2,2048,512]{2,0,1:T(2,128)(2,1)S(1)} %bitcast.9) | data formatting | bytes 8388608 | tf_op jit(solution)/shard_map/transpose | solution.py:325
  3.5 0.9 %copy-done = bf16[2,2,128,2048]{3,2,1,0:T(8,128)(2,1)S(1)} copy-done((bf16[2,2,128,2048]{3,2,1,0:T(8,128)(2,1)S(1)}, bf16[2,2,128,2048]{3,2,1,0:T(8,128)(2,1)}, u32[]{:S(2)}) %copy-start) | copy-done | bytes 2097176
  4.4 0.3 copy-done.1
  4.7 0.1 copy-done.2
  4.8 0.0 copy-done.3
  4.8 0.0 copy-done.4
  4.8 0.0 copy-done.5
  4.8 38.9 %shard_map.82 = f32[256,1024]{1,0:T(8,128)S(1)} custom-call(s32[4,64,2,512]{3,2,1,0:T(2,128)S(1)} %copy-done.1, s32[4,16,64]{2,1,0:T(8,128)S(1)} %bitcast.8, bf16[2,129]{1,0:T(2,128)(2,1)S(1)} %copy-done.5, bf16[2,4,64,64]{3,2,1,0:T(8,128)(2,1)S(1)} %copy-done.3, bf16[2,4,64,512]{3,2,1,0:T(8,128)(2,1)S(1)} %copy-done.2, bf16[4,512,512]{2,1,0:T(8,128)(2,1)S(1)} %bitcast.7, ...), custom_call_target="tpu_custom_call" | custom-call | tf_op jit(solution)/shard_map/pallas_call | solution.py:331
  43.7 1.9 %reshape.7 = f32[256,2,512]{2,1,0:T(2,128)} reshape(f32[256,1024]{1,0:T(8,128)S(1)} %shard_map.82) | data formatting | bytes 2097152 | tf_op jit(solution)/shard_map/reshape | solution.py:374
Async XLA Ops:
  0.0 2.8 %copy-start.6 = (bf16[2048,2,512]{2,1,0:T(2,128)(2,1)S(1)}, bf16[2048,2,512]{2,1,0:T(2,128)(2,1)}, u32[]{:S(2)}) copy-start(bf16[2048,2,512]{2,1,0:T(2,128)(2,1)} %param.15) | copy-start | bytes 12582916
  2.8 1.6 %copy-start = (bf16[2,2,128,2048]{3,2,1,0:T(8,128)(2,1)S(1)}, bf16[2,2,128,2048]{3,2,1,0:T(8,128)(2,1)}, u32[]{:S(2)}) copy-start(bf16[2,2,128,2048]{3,2,1,0:T(8,128)(2,1)} %u2_hbm.1) | copy-start | bytes 6291460
  2.8 1.9 %copy-start.1 = (s32[4,64,2,512]{3,2,1,0:T(2,128)S(1)}, s32[4,64,2,512]{3,2,1,0:T(2,128)}, u32[]{:S(2)}) copy-start(s32[4,64,2,512]{3,2,1,0:T(2,128)} %echoes.1) | copy-start | bytes 3145732
  2.8 2.0 %copy-start.2 = (bf16[2,4,64,512]{3,2,1,0:T(8,128)(2,1)S(1)}, bf16[2,4,64,512]{3,2,1,0:T(8,128)(2,1)}, u32[]{:S(2)}) copy-start(bf16[2,4,64,512]{3,2,1,0:T(8,128)(2,1)} %upsample1.1) | copy-start | bytes 1572868
  2.8 2.0 %copy-start.3 = (bf16[2,4,64,64]{3,2,1,0:T(8,128)(2,1)S(1)}, bf16[2,4,64,64]{3,2,1,0:T(8,128)(2,1)}, u32[]{:S(2)}) copy-start(bf16[2,4,64,64]{3,2,1,0:T(8,128)(2,1)} %interp0.1) | copy-start | bytes 196612
  2.8 2.0 %copy-start.4 = (s32[4,64,16]{1,2,0:T(8,128)S(1)}, s32[4,64,16]{1,2,0:T(8,128)}, u32[]{:S(2)}) copy-start(s32[4,64,16]{1,2,0:T(8,128)} %param.9) | copy-start | bytes 49156
  2.8 2.0 %copy-start.5 = (bf16[2,129]{1,0:T(2,128)(2,1)S(1)}, bf16[2,129]{1,0:T(2,128)(2,1)}, u32[]{:S(2)}) copy-start(bf16[2,129]{1,0:T(2,128)(2,1)} %replica.1) | copy-start | bytes 1552

commit v4 on v3

--- a/solution.py
+++ b/solution.py
@@ -48,8 +48,8 @@
 
 def kernel(
     dims, echoes, exponents, replica, interp0, upsample1, ph1, u2_hbm, ph2, out,
-    hp, u2, w0, w1, u2t, xs, halo_l, halo_r, band, rhs1, rhs2, u2m, pown, pms, pmr, ys, yr, lown, lmr, xsnd, xrcv, iown, y2s, y2r,
-    load_sem, u2_sem, halo_sem, core_sem, y_sem, l_sem, x_sem, y2_sem,
+    hp, u2, w0, w1, u2t, xs, halo_l, halo_r, band, rhs1, rhs2, u2m, pown, pms, pmr, ys, yr, lown, lmr, xsnd, xrcv, ysnd, yrcv, own_x, own_y, y2s, y2r, x2s, x2r,
+    load_sem, u2_sem, halo_sem, core_sem, y_sem, l_sem, x_sem, yf_sem, y2_sem, x2_sem,
 ):
     C, Y, Z, G, K, S, L, B0, nb, wedge, NB, half = dims
     W = CHUNK
@@ -148,9 +148,10 @@
         def _():
             xs[:, :, W + R : R + 2 * W] = jnp.zeros((2, S * L, W), jnp.bfloat16)
 
-    core_copy, y_copy, l_copy, x_copy, y2_copy = {}, {}, {}, {}, {}
+    core_copy, y_copy, l_copy, x_copy, yf_copy, y2_copy, x2_copy = {}, {}, {}, {}, {}, {}, {}
     u2_copy = remote(u2t.at[:, :, 1 - k], u2m, u2_sem, mate)
     sub = 64
+    hw = wedge // 2
 
     def turn_columns():
         load.wait()
@@ -225,51 +226,75 @@
             rhs2[g, : 2 * nb] = mixed(lown[nth, g])
             rhs2[g, 2 * nb :] = mixed(lmr[nth, g])
 
-        def block(e, d, store):
+        def block(e, d, stores):
             q = ((c + e) % C) * Y + (y + d) % Y
             values = [dot(jnp.concatenate([u2t[g, q, k], u2m[g, q]], axis=1), rhs2[g]) for g in range(G)]
-            for start in range(0, wedge, sub):
-                size = min(sub, wedge - start)
-                re = im = 0.0
-                for g in range(G):
-                    r, i = turned(values[g][start : start + size], ph2[g, q, k, start : start + size, lanes])
-                    re = re + r
-                    im = im + i
-                store[start : start + size, :W] = re.astype(store.dtype)
-                store[start : start + size, W:] = im.astype(store.dtype)
-
-        offsets = list(range(1, Y)) + [0]
+            for h, store in enumerate(stores):
+                for at in range(0, hw, sub):
+                    size = min(sub, hw - at)
+                    start = h * hw + at
+                    re = im = 0.0
+                    for g in range(G):
+                        r, i = turned(values[g][start : start + size], ph2[g, q, k, start : start + size, lanes])
+                        re = re + r
+                        im = im + i
+                    store[at : at + size, :W] = re.astype(store.dtype)
+                    store[at : at + size, W:] = im.astype(store.dtype)
+
+        for e in list(range(1, C)) + [0]:
+            for d in list(range(1, Y)) + [0]:
+                first = xsnd.at[nth, e - 1, d] if e else own_x.at[nth, d]
+                second = ysnd.at[nth, d - 1, e] if d else own_y.at[nth, e]
+                block(e, d, (first, second))
+                if e:
+                    at = (nth, e - 1, d)
+                    x_copy[nth, e, d] = remote(xsnd.at[at], xrcv.at[at], x_sem.at[at], x_peer(e))
+                    x_copy[nth, e, d].start()
+                if d:
+                    at = (nth, d - 1, e)
+                    yf_copy[nth, d, e] = remote(ysnd.at[at], yrcv.at[at], yf_sem.at[at], y_peer(d))
+                    yf_copy[nth, d, e].start()
+
+    def summed_x(nth, d):
+        total = own_x[nth, d]
         for e in range(1, C):
-            for d in offsets:
-                block(e, d, xsnd.at[nth, e - 1, d])
-                copy = remote(xsnd.at[nth, e - 1, d], xrcv.at[nth, e - 1, d], x_sem.at[nth, e - 1, d], x_peer(e))
-                copy.start()
-                x_copy[nth, e, d] = copy
-        for d in offsets:
-            block(0, d, iown.at[nth, d])
-
-    def sum_x(nth):
+            x_copy[nth, e, d].wait_recv()
+            total = total + xrcv[nth, e - 1, d].astype(jnp.float32)
+        return total
+
+    def summed_y(nth, e):
+        total = own_y[nth, e]
         for d in range(1, Y):
-            total = iown[nth, d]
-            for e in range(1, C):
-                x_copy[nth, e, d].wait_recv()
-                total = total + xrcv[nth, e - 1, d].astype(jnp.float32)
-            y2s[nth, d - 1] = total.astype(jnp.bfloat16)
-            copy = remote(y2s.at[nth, d - 1], y2r.at[nth, d - 1], y2_sem.at[nth, d - 1], y_peer(d))
-            copy.start()
-            y2_copy[nth, d] = copy
+            yf_copy[nth, d, e].wait_recv()
+            total = total + yrcv[nth, d - 1, e].astype(jnp.float32)
+        return total
+
+    def second_hop(nth):
+        for d in range(1, Y):
+            at = (nth, d - 1)
+            y2s[at] = summed_x(nth, d).astype(jnp.bfloat16)
+            y2_copy[nth, d] = remote(y2s.at[at], y2r.at[at], y2_sem.at[at], y_peer(d))
+            y2_copy[nth, d].start()
+        for e in range(1, C):
+            at = (nth, e - 1)
+            x2s[at] = summed_y(nth, e).astype(jnp.bfloat16)
+            x2_copy[nth, e] = remote(x2s.at[at], x2r.at[at], x2_sem.at[at], x_peer(e))
+            x2_copy[nth, e].start()
 
     def finish(j, nth):
+        lanes = pl.ds(j * W, W)
+        total = summed_x(nth, 0)
         for d in range(1, Y):
             y2_copy[nth, d].wait_recv()
-        total = iown[nth, 0]
+            total = total + y2r[nth, d - 1].astype(jnp.float32)
+        out[0, :hw, lanes] = total[:, :W]
+        out[1, :hw, lanes] = total[:, W:]
+        total = summed_y(nth, 0)
         for e in range(1, C):
-            x_copy[nth, e, 0].wait_recv()
-            total = total + xrcv[nth, e - 1, 0].astype(jnp.float32)
-        for d in range(1, Y):
-            total = total + y2r[nth, d - 1].astype(jnp.float32)
-        out[:, j * W : (j + 1) * W] = total[:, :W]
-        out[:, R + j * W : R + (j + 1) * W] = total[:, W:]
+            x2_copy[nth, e].wait_recv()
+            total = total + x2r[nth, e - 1].astype(jnp.float32)
+        out[0, hw:, lanes] = total[:, :W]
+        out[1, hw:, lanes] = total[:, W:]
 
     order = list(range(1, NB - 1)) + [0, NB - 1]
     for t in range(NB + 4):
@@ -286,12 +311,12 @@
         if 0 <= t - 1 < NB:
             level_two(order[t - 1], t - 1)
         if 0 <= t - 3 < NB:
-            sum_x(t - 3)
+            second_hop(t - 3)
         if 0 <= t - 4 < NB:
             finish(order[t - 4], t - 4)
 
     sent = [u2_copy]
-    for group in (core_copy, y_copy, l_copy, x_copy, y2_copy):
+    for group in (core_copy, y_copy, l_copy, x_copy, yf_copy, y2_copy, x2_copy):
         sent.extend(group.values())
     for copy in sent:
         copy.wait_send()
@@ -318,6 +343,7 @@
     wedge = B2 // (C * F)
     W = CHUNK
     NB = R // W
+    hw = wedge // 2
     half = (replica.shape[1] - 1) // 2
     bf16, f32 = jnp.bfloat16, jnp.float32
 
@@ -328,9 +354,9 @@
     dma = pltpu.SemaphoreType.DMA
     vm = pltpu.VMEM
     spec = pl.BlockSpec(memory_space=pltpu.VMEM)
-    flat = pl.pallas_call(
+    planes = pl.pallas_call(
         functools.partial(kernel, dims),
-        out_shape=jax.ShapeDtypeStruct((wedge, 2 * R), f32),
+        out_shape=jax.ShapeDtypeStruct((2, wedge, R), f32),
         in_specs=[spec] * 6 + [pl.BlockSpec(memory_space=pl.ANY), spec],
         out_specs=spec,
         scratch_shapes=[
@@ -353,11 +379,16 @@
             vm((NB, Y - 1, G, nb, 2 * W), bf16),
             vm((NB, G, nb, 2 * W), bf16),
             vm((NB, G, nb, 2 * W), bf16),
-            vm((NB, C - 1, Y, wedge, 2 * W), bf16),
-            vm((NB, C - 1, Y, wedge, 2 * W), bf16),
-            vm((NB, Y, wedge, 2 * W), f32),
-            vm((NB, Y - 1, wedge, 2 * W), bf16),
-            vm((NB, Y - 1, wedge, 2 * W), bf16),
+            vm((NB, C - 1, Y, hw, 2 * W), bf16),
+            vm((NB, C - 1, Y, hw, 2 * W), bf16),
+            vm((NB, Y - 1, C, hw, 2 * W), bf16),
+            vm((NB, Y - 1, C, hw, 2 * W), bf16),
+            vm((NB, Y, hw, 2 * W), f32),
+            vm((NB, C, hw, 2 * W), f32),
+            vm((NB, Y - 1, hw, 2 * W), bf16),
+            vm((NB, Y - 1, hw, 2 * W), bf16),
+            vm((NB, C - 1, hw, 2 * W), bf16),
+            vm((NB, C - 1, hw, 2 * W), bf16),
             dma((1,)),
             dma((2,)),
             dma((2, 2)),
@@ -365,13 +396,15 @@
             dma((NB, Y - 1, 2)),
             dma((NB, 2)),
             dma((NB, C - 1, Y, 2)),
+            dma((NB, Y - 1, C, 2)),
             dma((NB, Y - 1, 2)),
+            dma((NB, C - 1, 2)),
         ],
         compiler_params=pltpu.CompilerParams(
             collective_id=0, has_side_effects=True, vmem_limit_bytes=28 * 1024 * 1024
         ),
     )(echoes, exponents.transpose(0, 2, 1), replica, interp0, upsample1, ph1, upsample2, ph2)
-    return flat.reshape(wedge, 2, R)
+    return planes.transpose(1, 0, 2)
 
 
 def solution(mesh):

time: 45.7 us -> 46.1 us (level)
  Pallas kernels: 38.9 us -> 39.4 us
    reshape x1 -> x0, local copies, waits for them, and re-layouts: 1.86 us -> none  [shards(): return flat.reshape(wedge, 2, R)]
    transpose x0 -> x1, local copies, waits for them, and re-layouts: none -> 1.78 us  [shards(): return planes.transpose(1, 0, 2)]
where the time goes in v4:
time: 46.1 us; the launch traced here: 46 us
  Pallas kernels  39.4 us (85%)
  local copies, waits for them, and re-layouts  6.57 us (14%)
    pallas_call x1, Pallas kernels, shards(): pl.pallas_call(functools.partial(kernel, dims), out_shape=jax.ShapeDtypeS...  39.4 us
    unnamed x15, local copies, waits for them, and re-layouts  4.12 us
    transpose x1, local copies, waits for them, and re-layouts, shards(): return planes.transpose(1, 0, 2)  1.78 us

profile of v4, /device:TPU:0, one launch (start us, length us, event | category | flops | bytes accessed | tf_op | source)
XLA Modules:
  0.0 46.0 jit_solution(18173215765440910132)
XLA Ops:
  0.0 0.0 copy-start.6
  0.0 2.1 %copy.13 = bf16[512,4,512]{2,0,1:T(8,128)(2,1)S(1)} copy(bf16[512,4,512]{2,1,0:T(4,128)(2,1)} %param.13) | data formatting | bytes 4194304 | tf_op args[5]
  2.2 0.7 %copy-done.6 = bf16[2048,2,512]{2,1,0:T(2,128)(2,1)S(1)} copy-done((bf16[2048,2,512]{2,1,0:T(2,128)(2,1)S(1)}, bf16[2048,2,512]{2,1,0:T(2,128)(2,1)}, u32[]{:S(2)}) %copy-start.6) | copy-done | bytes 4194328
  2.8 0.0 copy-start
  2.8 0.0 copy-start.1
  2.8 0.0 copy-start.2
  2.8 0.0 copy-start.3
  2.8 0.0 copy-start.4
  2.8 0.0 copy-start.5
  2.9 0.7 %copy.10 = bf16[2,2048,512]{2,1,0:T(8,128)(2,1)S(1)} copy(bf16[2,2048,512]{2,0,1:T(2,128)(2,1)S(1)} %bitcast.11) | data formatting | bytes 8388608 | tf_op jit(solution)/shard_map/transpose | solution.py:351
  3.5 0.9 %copy-done = bf16[2,2,128,2048]{3,2,1,0:T(8,128)(2,1)S(1)} copy-done((bf16[2,2,128,2048]{3,2,1,0:T(8,128)(2,1)S(1)}, bf16[2,2,128,2048]{3,2,1,0:T(8,128)(2,1)}, u32[]{:S(2)}) %copy-start) | copy-done | bytes 2097176
  4.4 0.3 copy-done.1
  4.7 0.1 copy-done.2
  4.8 0.0 copy-done.3
  4.8 0.0 copy-done.4
  4.8 0.0 copy-done.5
  4.8 39.4 %shard_map.82 = f32[2,256,512]{2,1,0:T(8,128)S(1)} custom-call(s32[4,64,2,512]{3,2,1,0:T(2,128)S(1)} %copy-done.1, s32[4,16,64]{2,1,0:T(8,128)S(1)} %bitcast.10, bf16[2,129]{1,0:T(2,128)(2,1)S(1)} %copy-done.5, bf16[2,4,64,64]{3,2,1,0:T(8,128)(2,1)S(1)} %copy-done.3, bf16[2,4,64,512]{3,2,1,0:T(8,128)(2,1)S(1)} %copy-done.2, ...), custom_call_target="tpu_custom_call" | custom-call | tf_op jit(solution)/shard_map/pallas_call | solution.py:357
  44.2 1.8 %copy.11 = f32[256,2,512]{2,1,0:T(2,128)} copy(f32[256,2,512]{2,0,1:T(8,128)S(1)} %bitcast.9) | data formatting | bytes 2097152 | tf_op jit(solution)/shard_map/transpose | solution.py:407
Async XLA Ops:
  0.0 2.8 %copy-start.6 = (bf16[2048,2,512]{2,1,0:T(2,128)(2,1)S(1)}, bf16[2048,2,512]{2,1,0:T(2,128)(2,1)}, u32[]{:S(2)}) copy-start(bf16[2048,2,512]{2,1,0:T(2,128)(2,1)} %param.15) | copy-start | bytes 12582916
  2.8 1.6 %copy-start = (bf16[2,2,128,2048]{3,2,1,0:T(8,128)(2,1)S(1)}, bf16[2,2,128,2048]{3,2,1,0:T(8,128)(2,1)}, u32[]{:S(2)}) copy-start(bf16[2,2,128,2048]{3,2,1,0:T(8,128)(2,1)} %u2_hbm.1) | copy-start | bytes 6291460
  2.8 1.9 %copy-start.1 = (s32[4,64,2,512]{3,2,1,0:T(2,128)S(1)}, s32[4,64,2,512]{3,2,1,0:T(2,128)}, u32[]{:S(2)}) copy-start(s32[4,64,2,512]{3,2,1,0:T(2,128)} %echoes.1) | copy-start | bytes 3145732
  2.8 2.0 %copy-start.2 = (bf16[2,4,64,512]{3,2,1,0:T(8,128)(2,1)S(1)}, bf16[2,4,64,512]{3,2,1,0:T(8,128)(2,1)}, u32[]{:S(2)}) copy-start(bf16[2,4,64,512]{3,2,1,0:T(8,128)(2,1)} %upsample1.1) | copy-start | bytes 1572868
  2.8 2.0 %copy-start.3 = (bf16[2,4,64,64]{3,2,1,0:T(8,128)(2,1)S(1)}, bf16[2,4,64,64]{3,2,1,0:T(8,128)(2,1)}, u32[]{:S(2)}) copy-start(bf16[2,4,64,64]{3,2,1,0:T(8,128)(2,1)} %interp0.1) | copy-start | bytes 196612
  2.8 2.0 %copy-start.4 = (s32[4,64,16]{1,2,0:T(8,128)S(1)}, s32[4,64,16]{1,2,0:T(8,128)}, u32[]{:S(2)}) copy-start(s32[4,64,16]{1,2,0:T(8,128)} %param.9) | copy-start | bytes 49156
  2.8 2.0 %copy-start.5 = (bf16[2,129]{1,0:T(2,128)(2,1)S(1)}, bf16[2,129]{1,0:T(2,128)(2,1)}, u32[]{:S(2)}) copy-start(bf16[2,129]{1,0:T(2,128)(2,1)} %replica.1) | copy-start | bytes 1552

commit v5 on v4

--- a/solution.py
+++ b/solution.py
@@ -48,7 +48,7 @@
 
 def kernel(
     dims, echoes, exponents, replica, interp0, upsample1, ph1, u2_hbm, ph2, out,
-    hp, u2, w0, w1, u2t, xs, halo_l, halo_r, band, rhs1, rhs2, u2m, pown, pms, pmr, ys, yr, lown, lmr, xsnd, xrcv, ysnd, yrcv, own_x, own_y, y2s, y2r, x2s, x2r,
+    hp, u2, w0, w1, u2t, xs, halo_l, halo_r, band, rhs1, rhs2, u2m, pown, pms, pmr, ys, yr, lown, lmr, snd, xrcv, yrcv, own, y2s, y2r, x2s, x2r,
     load_sem, u2_sem, halo_sem, core_sem, y_sem, l_sem, x_sem, yf_sem, y2_sem, x2_sem,
 ):
     C, Y, Z, G, K, S, L, B0, nb, wedge, NB, half = dims
@@ -156,12 +156,17 @@
     def turn_columns():
         load.wait()
         step = max(wedge, W)
-        for g in range(G):
-            for first in range(0, u2.shape[3], step):
-                block = u2[g, :, :, first : first + step].reshape(2 * nb, step).T
-                for i in range(step // wedge):
-                    q = first // wedge + i
-                    u2t[g, q // 2, q % 2] = block[i * wedge : (i + 1) * wedge]
+        steps = u2.shape[3] // step
+
+        @pl.loop(0, G * steps)
+        def _(t):
+            g = t // steps
+            first = pl.multiple_of((t % steps) * step, step)
+            block = u2[g, :, :, pl.ds(first, step)].reshape(2 * nb, step).T
+            for i in range(step // wedge):
+                q = (t % steps) * (step // wedge) + i
+                u2t[g, q // 2, q % 2] = block[i * wedge : (i + 1) * wedge]
+
         u2_copy.start()
 
     def level_one(j, nth):
@@ -171,9 +176,12 @@
         for s in range(S):
             beams = dot(w0[s], mixed(comp[s * L : (s + 1) * L])).astype(jnp.bfloat16)
             rhs1[s] = mixed(beams)
-        def block(core, d, store):
-            base = pl.multiple_of((((y + d) % Y) * 2 + core) * nb, nb)
-            for g in range(G):
+        def blocks(core, store):
+            @pl.loop(0, Y * G)
+            def _(t):
+                d = t // G
+                g = t % G
+                base = pl.multiple_of((((y + d) % Y) * 2 + core) * nb, nb)
                 values = [dot(w1[g * K + kid, pl.ds(base, nb), :], rhs1[g * K + kid]) for kid in range(K)]
                 for start in range(0, nb, sub):
                     size = min(sub, nb - start)
@@ -183,17 +191,15 @@
                         r, i = turned(values[kid][start : start + size], ph1[g * K + kid, rows, lanes])
                         re = re + r
                         im = im + i
-                    store[g, start : start + size, :W] = re.astype(store.dtype)
-                    store[g, start : start + size, W:] = im.astype(store.dtype)
-
-        offsets = list(range(1, Y)) + [0]
-        for d in offsets:
-            block(1 - k, d, pms.at[nth, d])
+                    store[d, g, start : start + size, :W] = re.astype(store.dtype)
+                    store[d, g, start : start + size, W:] = im.astype(store.dtype)
+
+        blocks(1 - k, pms.at[nth])
+        for d in range(Y):
             copy = remote(pms.at[nth, d], pmr.at[nth, d], core_sem.at[nth, d], mate)
             copy.start()
             core_copy[nth, d] = copy
-        for d in offsets:
-            block(k, d, pown.at[nth, d])
+        blocks(k, pown.at[nth])
 
     def sum_cores(nth):
         for d in range(1, Y):
@@ -226,10 +232,13 @@
             rhs2[g, : 2 * nb] = mixed(lown[nth, g])
             rhs2[g, 2 * nb :] = mixed(lmr[nth, g])
 
-        def block(e, d, stores):
+        @pl.loop(0, C * Y)
+        def _(t):
+            e = t // Y
+            d = t % Y
             q = ((c + e) % C) * Y + (y + d) % Y
             values = [dot(jnp.concatenate([u2t[g, q, k], u2m[g, q]], axis=1), rhs2[g]) for g in range(G)]
-            for h, store in enumerate(stores):
+            for h in range(2):
                 for at in range(0, hw, sub):
                     size = min(sub, hw - at)
                     start = h * hw + at
@@ -238,32 +247,31 @@
                         r, i = turned(values[g][start : start + size], ph2[g, q, k, start : start + size, lanes])
                         re = re + r
                         im = im + i
-                    store[at : at + size, :W] = re.astype(store.dtype)
-                    store[at : at + size, W:] = im.astype(store.dtype)
+                    own[nth, h, e, d, at : at + size, :W] = re
+                    own[nth, h, e, d, at : at + size, W:] = im
+                    snd[nth, h, e, d, at : at + size, :W] = re.astype(jnp.bfloat16)
+                    snd[nth, h, e, d, at : at + size, W:] = im.astype(jnp.bfloat16)
 
         for e in list(range(1, C)) + [0]:
             for d in list(range(1, Y)) + [0]:
-                first = xsnd.at[nth, e - 1, d] if e else own_x.at[nth, d]
-                second = ysnd.at[nth, d - 1, e] if d else own_y.at[nth, e]
-                block(e, d, (first, second))
                 if e:
                     at = (nth, e - 1, d)
-                    x_copy[nth, e, d] = remote(xsnd.at[at], xrcv.at[at], x_sem.at[at], x_peer(e))
+                    x_copy[nth, e, d] = remote(snd.at[nth, 0, e, d], xrcv.at[at], x_sem.at[at], x_peer(e))
                     x_copy[nth, e, d].start()
                 if d:
                     at = (nth, d - 1, e)
-                    yf_copy[nth, d, e] = remote(ysnd.at[at], yrcv.at[at], yf_sem.at[at], y_peer(d))
+                    yf_copy[nth, d, e] = remote(snd.at[nth, 1, e, d], yrcv.at[at], yf_sem.at[at], y_peer(d))
                     yf_copy[nth, d, e].start()
 
     def summed_x(nth, d):
-        total = own_x[nth, d]
+        total = own[nth, 0, 0, d]
         for e in range(1, C):
             x_copy[nth, e, d].wait_recv()
             total = total + xrcv[nth, e - 1, d].astype(jnp.float32)
         return total
 
     def summed_y(nth, e):
-        total = own_y[nth, e]
+        total = own[nth, 1, e, 0]
         for d in range(1, Y):
             yf_copy[nth, d, e].wait_recv()
             total = total + yrcv[nth, d - 1, e].astype(jnp.float32)
@@ -302,12 +310,12 @@
             if order[t] == 0:
                 fill_halo()
             level_one(order[t], t)
-        if t == 0:
-            turn_columns()
         if 0 <= t - 1 < NB:
             sum_y(t - 1)
         if t < NB:
             sum_cores(t)
+        if t == 0:
+            turn_columns()
         if 0 <= t - 1 < NB:
             level_two(order[t - 1], t - 1)
         if 0 <= t - 3 < NB:
@@ -379,12 +387,10 @@
             vm((NB, Y - 1, G, nb, 2 * W), bf16),
             vm((NB, G, nb, 2 * W), bf16),
             vm((NB, G, nb, 2 * W), bf16),
-            vm((NB, C - 1, Y, hw, 2 * W), bf16),
+            vm((NB, 2, C, Y, hw, 2 * W), bf16),
             vm((NB, C - 1, Y, hw, 2 * W), bf16),
             vm((NB, Y - 1, C, hw, 2 * W), bf16),
-            vm((NB, Y - 1, C, hw, 2 * W), bf16),
-            vm((NB, Y, hw, 2 * W), f32),
-            vm((NB, C, hw, 2 * W), f32),
+            vm((NB, 2, C, Y, hw, 2 * W), f32),
             vm((NB, Y - 1, hw, 2 * W), bf16),
             vm((NB, Y - 1, hw, 2 * W), bf16),
             vm((NB, C - 1, hw, 2 * W), bf16),
@@ -401,7 +407,7 @@
             dma((NB, C - 1, 2)),
         ],
         compiler_params=pltpu.CompilerParams(
-            collective_id=0, has_side_effects=True, vmem_limit_bytes=28 * 1024 * 1024
+            collective_id=0, has_side_effects=True, vmem_limit_bytes=32 * 1024 * 1024
         ),
     )(echoes, exponents.transpose(0, 2, 1), replica, interp0, upsample1, ph1, upsample2, ph2)
     return planes.transpose(1, 0, 2)

time: 46.1 us -> 48.6 us (1.054)
  Pallas kernels: 39.4 us -> 41.8 us
    pallas_call x1, Pallas kernels: 39.4 us -> 41.8 us  [shards(): pl.pallas_call(functools.partial(kernel, dims), out_shape=jax.ShapeDtypeS...]
where the time goes in v5:
time: 48.6 us; the launch traced here: 48.5 us
  Pallas kernels  41.8 us (86%)
  local copies, waits for them, and re-layouts  6.57 us (14%)
    pallas_call x1, Pallas kernels, shards(): pl.pallas_call(functools.partial(kernel, dims), out_shape=jax.ShapeDtypeS...  41.8 us
    unnamed x15, local copies, waits for them, and re-layouts  4.12 us
    transpose x1, local copies, waits for them, and re-layouts, shards(): return planes.transpose(1, 0, 2)  1.78 us

profile of v5, /device:TPU:0, one launch (start us, length us, event | category | flops | bytes accessed | tf_op | source)
XLA Modules:
  0.0 48.5 jit_solution(2789977629469061619)
XLA Ops:
  0.0 0.0 copy-start.6
  0.0 2.1 %copy.13 = bf16[512,4,512]{2,0,1:T(8,128)(2,1)S(1)} copy(bf16[512,4,512]{2,1,0:T(4,128)(2,1)} %param.13) | data formatting | bytes 4194304 | tf_op args[5]
  2.2 0.7 %copy-done.6 = bf16[2048,2,512]{2,1,0:T(2,128)(2,1)S(1)} copy-done((bf16[2048,2,512]{2,1,0:T(2,128)(2,1)S(1)}, bf16[2048,2,512]{2,1,0:T(2,128)(2,1)}, u32[]{:S(2)}) %copy-start.6) | copy-done | bytes 4194328
  2.8 0.0 copy-start
  2.8 0.0 copy-start.1
  2.8 0.0 copy-start.2
  2.8 0.0 copy-start.3
  2.8 0.0 copy-start.4
  2.8 0.0 copy-start.5
  2.9 0.7 %copy.10 = bf16[2,2048,512]{2,1,0:T(8,128)(2,1)S(1)} copy(bf16[2,2048,512]{2,0,1:T(2,128)(2,1)S(1)} %bitcast.11) | data formatting | bytes 8388608 | tf_op jit(solution)/shard_map/transpose | solution.py:359
  3.5 0.9 %copy-done = bf16[2,2,128,2048]{3,2,1,0:T(8,128)(2,1)S(1)} copy-done((bf16[2,2,128,2048]{3,2,1,0:T(8,128)(2,1)S(1)}, bf16[2,2,128,2048]{3,2,1,0:T(8,128)(2,1)}, u32[]{:S(2)}) %copy-start) | copy-done | bytes 2097176
  4.4 0.3 copy-done.1
  4.7 0.1 copy-done.2
  4.8 0.0 copy-done.3
  4.8 0.0 copy-done.4
  4.8 0.0 copy-done.5
  4.8 41.8 %shard_map.82 = f32[2,256,512]{2,1,0:T(8,128)S(1)} custom-call(s32[4,64,2,512]{3,2,1,0:T(2,128)S(1)} %copy-done.1, s32[4,16,64]{2,1,0:T(8,128)S(1)} %bitcast.10, bf16[2,129]{1,0:T(2,128)(2,1)S(1)} %copy-done.5, bf16[2,4,64,64]{3,2,1,0:T(8,128)(2,1)S(1)} %copy-done.3, bf16[2,4,64,512]{3,2,1,0:T(8,128)(2,1)S(1)} %copy-done.2, ...), custom_call_target="tpu_custom_call" | custom-call | tf_op jit(solution)/shard_map/pallas_call | solution.py:365
  46.7 1.8 %copy.11 = f32[256,2,512]{2,1,0:T(2,128)} copy(f32[256,2,512]{2,0,1:T(8,128)S(1)} %bitcast.9) | data formatting | bytes 2097152 | tf_op jit(solution)/shard_map/transpose | solution.py:413
Async XLA Ops:
  0.0 2.8 %copy-start.6 = (bf16[2048,2,512]{2,1,0:T(2,128)(2,1)S(1)}, bf16[2048,2,512]{2,1,0:T(2,128)(2,1)}, u32[]{:S(2)}) copy-start(bf16[2048,2,512]{2,1,0:T(2,128)(2,1)} %param.15) | copy-start | bytes 12582916
  2.8 1.6 %copy-start = (bf16[2,2,128,2048]{3,2,1,0:T(8,128)(2,1)S(1)}, bf16[2,2,128,2048]{3,2,1,0:T(8,128)(2,1)}, u32[]{:S(2)}) copy-start(bf16[2,2,128,2048]{3,2,1,0:T(8,128)(2,1)} %u2_hbm.1) | copy-start | bytes 6291460
  2.8 1.9 %copy-start.1 = (s32[4,64,2,512]{3,2,1,0:T(2,128)S(1)}, s32[4,64,2,512]{3,2,1,0:T(2,128)}, u32[]{:S(2)}) copy-start(s32[4,64,2,512]{3,2,1,0:T(2,128)} %echoes.1) | copy-start | bytes 3145732
  2.8 2.0 %copy-start.2 = (bf16[2,4,64,512]{3,2,1,0:T(8,128)(2,1)S(1)}, bf16[2,4,64,512]{3,2,1,0:T(8,128)(2,1)}, u32[]{:S(2)}) copy-start(bf16[2,4,64,512]{3,2,1,0:T(8,128)(2,1)} %upsample1.1) | copy-start | bytes 1572868
  2.8 2.0 %copy-start.3 = (bf16[2,4,64,64]{3,2,1,0:T(8,128)(2,1)S(1)}, bf16[2,4,64,64]{3,2,1,0:T(8,128)(2,1)}, u32[]{:S(2)}) copy-start(bf16[2,4,64,64]{3,2,1,0:T(8,128)(2,1)} %interp0.1) | copy-start | bytes 196612
  2.8 2.0 %copy-start.4 = (s32[4,64,16]{1,2,0:T(8,128)S(1)}, s32[4,64,16]{1,2,0:T(8,128)}, u32[]{:S(2)}) copy-start(s32[4,64,16]{1,2,0:T(8,128)} %param.9) | copy-start | bytes 49156
  2.8 2.0 %copy-start.5 = (bf16[2,129]{1,0:T(2,128)(2,1)S(1)}, bf16[2,129]{1,0:T(2,128)(2,1)}, u32[]{:S(2)}) copy-start(bf16[2,129]{1,0:T(2,128)(2,1)} %replica.1) | copy-start | bytes 1552

commit v6 on v4

--- a/solution.py
+++ b/solution.py
@@ -150,7 +150,7 @@
 
     core_copy, y_copy, l_copy, x_copy, yf_copy, y2_copy, x2_copy = {}, {}, {}, {}, {}, {}, {}
     u2_copy = remote(u2t.at[:, :, 1 - k], u2m, u2_sem, mate)
-    sub = 64
+    sub = 32
     hw = wedge // 2
 
     def turn_columns():
@@ -302,12 +302,12 @@
             if order[t] == 0:
                 fill_halo()
             level_one(order[t], t)
-        if t == 0:
-            turn_columns()
         if 0 <= t - 1 < NB:
             sum_y(t - 1)
         if t < NB:
             sum_cores(t)
+        if t == 0:
+            turn_columns()
         if 0 <= t - 1 < NB:
             level_two(order[t - 1], t - 1)
         if 0 <= t - 3 < NB:

time: 46.1 us -> 46.4 us (level)
  no operation moved by 1% of the time
where the time goes in v6:
time: 46.4 us; the launch traced here: 46.2 us
  Pallas kernels  39.6 us (85%)
  local copies, waits for them, and re-layouts  6.57 us (14%)
    pallas_call x1, Pallas kernels, shards(): pl.pallas_call(functools.partial(kernel, dims), out_shape=jax.ShapeDtypeS...  39.6 us
    unnamed x15, local copies, waits for them, and re-layouts  4.12 us
    transpose x1, local copies, waits for them, and re-layouts, shards(): return planes.transpose(1, 0, 2)  1.78 us

profile of v6, /device:TPU:0, one launch (start us, length us, event | category | flops | bytes accessed | tf_op | source)
XLA Modules:
  0.0 46.2 jit_solution(13943962335686011716)
XLA Ops:
  0.0 0.0 copy-start.6
  0.0 2.1 %copy.13 = bf16[512,4,512]{2,0,1:T(8,128)(2,1)S(1)} copy(bf16[512,4,512]{2,1,0:T(4,128)(2,1)} %param.13) | data formatting | bytes 4194304 | tf_op args[5]
  2.2 0.7 %copy-done.6 = bf16[2048,2,512]{2,1,0:T(2,128)(2,1)S(1)} copy-done((bf16[2048,2,512]{2,1,0:T(2,128)(2,1)S(1)}, bf16[2048,2,512]{2,1,0:T(2,128)(2,1)}, u32[]{:S(2)}) %copy-start.6) | copy-done | bytes 4194328
  2.8 0.0 copy-start
  2.8 0.0 copy-start.1
  2.8 0.0 copy-start.2
  2.8 0.0 copy-start.3
  2.8 0.0 copy-start.4
  2.8 0.0 copy-start.5
  2.9 0.7 %copy.10 = bf16[2,2048,512]{2,1,0:T(8,128)(2,1)S(1)} copy(bf16[2,2048,512]{2,0,1:T(2,128)(2,1)S(1)} %bitcast.11) | data formatting | bytes 8388608 | tf_op jit(solution)/shard_map/transpose | solution.py:351
  3.5 0.9 %copy-done = bf16[2,2,128,2048]{3,2,1,0:T(8,128)(2,1)S(1)} copy-done((bf16[2,2,128,2048]{3,2,1,0:T(8,128)(2,1)S(1)}, bf16[2,2,128,2048]{3,2,1,0:T(8,128)(2,1)}, u32[]{:S(2)}) %copy-start) | copy-done | bytes 2097176
  4.4 0.3 copy-done.1
  4.7 0.1 copy-done.2
  4.8 0.0 copy-done.3
  4.8 0.0 copy-done.4
  4.8 0.0 copy-done.5
  4.8 39.6 %shard_map.82 = f32[2,256,512]{2,1,0:T(8,128)S(1)} custom-call(s32[4,64,2,512]{3,2,1,0:T(2,128)S(1)} %copy-done.1, s32[4,16,64]{2,1,0:T(8,128)S(1)} %bitcast.10, bf16[2,129]{1,0:T(2,128)(2,1)S(1)} %copy-done.5, bf16[2,4,64,64]{3,2,1,0:T(8,128)(2,1)S(1)} %copy-done.3, bf16[2,4,64,512]{3,2,1,0:T(8,128)(2,1)S(1)} %copy-done.2, ...), custom_call_target="tpu_custom_call" | custom-call | tf_op jit(solution)/shard_map/pallas_call | solution.py:357
  44.4 1.8 %copy.11 = f32[256,2,512]{2,1,0:T(2,128)} copy(f32[256,2,512]{2,0,1:T(8,128)S(1)} %bitcast.9) | data formatting | bytes 2097152 | tf_op jit(solution)/shard_map/transpose | solution.py:407
Async XLA Ops:
  0.0 2.8 %copy-start.6 = (bf16[2048,2,512]{2,1,0:T(2,128)(2,1)S(1)}, bf16[2048,2,512]{2,1,0:T(2,128)(2,1)}, u32[]{:S(2)}) copy-start(bf16[2048,2,512]{2,1,0:T(2,128)(2,1)} %param.15) | copy-start | bytes 12582916
  2.8 1.6 %copy-start = (bf16[2,2,128,2048]{3,2,1,0:T(8,128)(2,1)S(1)}, bf16[2,2,128,2048]{3,2,1,0:T(8,128)(2,1)}, u32[]{:S(2)}) copy-start(bf16[2,2,128,2048]{3,2,1,0:T(8,128)(2,1)} %u2_hbm.1) | copy-start | bytes 6291460
  2.8 1.9 %copy-start.1 = (s32[4,64,2,512]{3,2,1,0:T(2,128)S(1)}, s32[4,64,2,512]{3,2,1,0:T(2,128)}, u32[]{:S(2)}) copy-start(s32[4,64,2,512]{3,2,1,0:T(2,128)} %echoes.1) | copy-start | bytes 3145732
  2.8 2.0 %copy-start.2 = (bf16[2,4,64,512]{3,2,1,0:T(8,128)(2,1)S(1)}, bf16[2,4,64,512]{3,2,1,0:T(8,128)(2,1)}, u32[]{:S(2)}) copy-start(bf16[2,4,64,512]{3,2,1,0:T(8,128)(2,1)} %upsample1.1) | copy-start | bytes 1572868
  2.8 2.0 %copy-start.3 = (bf16[2,4,64,64]{3,2,1,0:T(8,128)(2,1)S(1)}, bf16[2,4,64,64]{3,2,1,0:T(8,128)(2,1)}, u32[]{:S(2)}) copy-start(bf16[2,4,64,64]{3,2,1,0:T(8,128)(2,1)} %interp0.1) | copy-start | bytes 196612
  2.8 2.0 %copy-start.4 = (s32[4,64,16]{1,2,0:T(8,128)S(1)}, s32[4,64,16]{1,2,0:T(8,128)}, u32[]{:S(2)}) copy-start(s32[4,64,16]{1,2,0:T(8,128)} %param.9) | copy-start | bytes 49156
  2.8 2.0 %copy-start.5 = (bf16[2,129]{1,0:T(2,128)(2,1)S(1)}, bf16[2,129]{1,0:T(2,128)(2,1)}, u32[]{:S(2)}) copy-start(bf16[2,129]{1,0:T(2,128)(2,1)} %replica.1) | copy-start | bytes 1552
